TPU v7x, 32 devices: a whole 2x2x4 slice. The times are simulated.
32 devices in a mesh: head: 8 (over z, x), dp: 4 (over y, core).
Axes of the slice: x: 2, y: 2, z: 4, core: 2. Of those that a mesh axis runs over, the one named last changes fastest.
Arguments:
- tokens: bfloat16 [8192, 1024], P('dp'), may hold values from -6 to 6
- cotangent: bfloat16 [8192, 1024], P('dp'), may hold values from -6 to 6
- group_ids: int32 [4], P('dp'), may hold values from 0 to 7
- group_weights: float32 [8], replicated, may hold values from 0.25 to 2
- gain_attn: float32 [1024], replicated, may hold values from 0.5 to 1.5
- w_query: bfloat16 [1024, 1024], P(None, 'head'), may hold values from -0.1875 to 0.1875
- w_latent: bfloat16 [1024, 512], replicated, may hold values from -0.1875 to 0.1875
- w_key: bfloat16 [256, 1024], P(None, 'head'), may hold values from -0.375 to 0.375
- w_value: bfloat16 [256, 1024], P(None, 'head'), may hold values from -0.375 to 0.375
- w_out: bfloat16 [1024, 1024], P('head'), may hold values from -1.5 to 1.5
- gain_mlp: float32 [1024], replicated, may hold values from 0.5 to 1.5
- w_gate: bfloat16 [1024, 2816], P(None, 'head'), may hold values from -0.1875 to 0.1875
- w_up: bfloat16 [1024, 2816], P(None, 'head'), may hold values from -0.1875 to 0.1875
- w_down: bfloat16 [2816, 1024], P('head'), may hold values from -0.109375 to 0.109375
Outputs:
- block_out: bfloat16 [8192, 1024], P('dp')
- grad_tokens: bfloat16 [8192, 1024], P('dp')
- grad_gain_attn: float32 [1024], P('dp')
- grad_w_query: float32 [1024, 1024], P('dp', 'head')
- grad_w_latent: float32 [1024, 512], P('dp', 'head')
- grad_w_key: float32 [256, 1024], P('dp', 'head')
- grad_w_value: float32 [256, 1024], P('dp', 'head')
- grad_w_out: float32 [1024, 1024], P('head', 'dp')
- grad_gain_mlp: float32 [1024], P('dp')
- grad_w_gate: float32 [1024, 2816], P('dp', 'head')
- grad_w_up: float32 [1024, 2816], P('dp', 'head')
- grad_w_down: float32 [2816, 1024], P('head', 'dp')
All inputs are finite; a program needn't handle non-finite values.
Results may differ from a plain program's by a relative error of at most 0.025.
Values may be sent and summed in bfloat16 or wider, within the bound.
No kernel may reach another device: no remote copies, remote signals or barrier semaphores. Data moves between devices by JAX's collectives and lax.ppermute only.
A program may use at most 192 MiB of HBM per device.

v0:
```python
import jax
import jax.numpy as jnp
from jax import lax
from jax.sharding import PartitionSpec as P

HD = 64
BLOCK = 512


epsilon = 1e-05
negative = -1e30


def partner(block, axis, bit):
    count = lax.axis_size(axis)
    route = []
    for low in range(count):
        high = low | 1 << bit
        if high != low and high < count:
            route += [(low, high), (high, low)]
    return lax.ppermute(block, axis, route)


def rms_gain(values_in, gain_vec):
    return (
        values_in
        * lax.rsqrt(jnp.mean(values_in * values_in, axis=-1, keepdims=True) + epsilon)
        * gain_vec
    )


def gated(gate_proj, up_proj):
    return jax.nn.silu(gate_proj) * up_proj


def product(left, right):
    return jnp.dot(left, right, preferred_element_type=jnp.float32)


def contract_rows(left, right):
    return lax.dot_general(
        left, right, (((0,), (0,)), ((), ())), preferred_element_type=jnp.float32
    )


def contract_last(left, right):
    return lax.dot_general(
        left, right, (((1,), (1,)), ((), ())), preferred_element_type=jnp.float32
    )


def masked_scores(query_block, key_all, first_row, score_scale):
    raw_scores = jnp.einsum(
        "qhe,khe->hqk", query_block, key_all, preferred_element_type=jnp.float32
    )
    grid_shape = (query_block.shape[0], key_all.shape[0])
    row_ids = first_row + lax.broadcasted_iota(jnp.int32, grid_shape, 0)
    col_ids = lax.broadcasted_iota(jnp.int32, grid_shape, 1)
    return jnp.where((col_ids <= row_ids)[None], raw_scores * score_scale, negative)


def body(
    tokens,
    cotangent,
    group_ids,
    group_weights,
    gain_attn,
    w_query,
    w_latent,
    w_key,
    w_value,
    w_out,
    gain_mlp,
    w_gate,
    w_up,
    w_down,
):
    model_width = tokens.shape[1]
    latent_width = w_key.shape[0]
    local_cols = w_query.shape[1]
    heads_here = local_cols // HD
    seq_count = group_ids.shape[0]
    length = tokens.shape[0] // seq_count
    blocks = length // BLOCK
    score_scale = HD ** (-0.5)
    half_size = lax.axis_size("head") // 2
    latent_index = lax.axis_index("head") // half_size
    w_lat = lax.dynamic_slice_in_dim(w_latent, latent_index * latent_width, latent_width, 1)
    inputs = tokens.astype(jnp.float32)
    normed = rms_gain(inputs, gain_attn).astype(jnp.bfloat16)
    queries = product(normed, w_query).astype(jnp.bfloat16)
    latent_state = product(normed, w_lat).astype(jnp.bfloat16)
    keys = product(latent_state, w_key).astype(jnp.bfloat16)
    values = product(latent_state, w_value).astype(jnp.bfloat16)
    head_shape = (seq_count, length, heads_here, HD)
    query_seq = queries.reshape(head_shape)
    key_seq = keys.reshape(head_shape)
    value_seq = values.reshape(head_shape)

    def forward_block(index):
        sequence = index // blocks
        first_row = index % blocks * BLOCK
        query_all = lax.dynamic_index_in_dim(query_seq, sequence, 0, keepdims=False)
        key_all = lax.dynamic_index_in_dim(key_seq, sequence, 0, keepdims=False)
        value_all = lax.dynamic_index_in_dim(value_seq, sequence, 0, keepdims=False)
        query_block = lax.dynamic_slice_in_dim(query_all, first_row, BLOCK, 0)
        scores = masked_scores(query_block, key_all, first_row, score_scale)
        largest = jnp.max(scores, axis=-1, keepdims=True)
        exponent = jnp.exp(scores - largest)
        denominator = jnp.sum(exponent, axis=-1, keepdims=True)
        prob_low = (exponent / denominator).astype(jnp.bfloat16)
        mixed_block = jnp.einsum(
            "hqk,khe->qhe", prob_low, value_all, preferred_element_type=jnp.float32
        )
        mixed_block = mixed_block.astype(jnp.bfloat16).reshape(BLOCK, local_cols)
        log_total = (largest + jnp.log(denominator))[..., 0]
        return (mixed_block, log_total, log_total)

    mixed_blocks, log_totals, summed_blocks = lax.map(
        forward_block, jnp.arange(seq_count * blocks, dtype=jnp.int32)
    )
    mixed = mixed_blocks.reshape(seq_count * length, local_cols)
    attn_sum = lax.psum(product(mixed, w_out).astype(jnp.bfloat16), "head").astype(jnp.float32)
    hidden_state = inputs + attn_sum
    normed2 = rms_gain(hidden_state, gain_mlp).astype(jnp.bfloat16)
    gate_proj = product(normed2, w_gate)
    up_proj = product(normed2, w_up)
    activated = gated(gate_proj, up_proj).astype(jnp.bfloat16)
    mlp_sum = lax.psum(product(activated, w_down).astype(jnp.bfloat16), "head").astype(jnp.float32)
    block_out = (hidden_state + mlp_sum).astype(jnp.bfloat16)
    labels = jnp.arange(group_weights.shape[0], dtype=jnp.int32)
    row_weight = jnp.sum(
        jnp.where(group_ids[:, None] == labels[None, :], group_weights[None, :], 0.0), axis=1
    )
    grad_out = (
        cotangent.astype(jnp.float32).reshape(seq_count, length, model_width)
        * row_weight[:, None, None]
    )
    grad_out = grad_out.reshape(seq_count * length, model_width)
    grad_low = grad_out.astype(jnp.bfloat16)
    grad_w_down = contract_rows(activated, grad_low)
    grad_act = contract_last(grad_low, w_down)
    unused_value, pull_gate = jax.vjp(gated, gate_proj, up_proj)
    grad_gate, up_projection_gradient = pull_gate(grad_act)
    grad_gate = grad_gate.astype(jnp.bfloat16)
    up_projection_gradient = up_projection_gradient.astype(jnp.bfloat16)
    grad_w_gate = contract_rows(normed2, grad_gate)
    grad_w_up = contract_rows(normed2, up_projection_gradient)
    grad_normed2 = lax.psum(
        (contract_last(grad_gate, w_gate) + contract_last(up_projection_gradient, w_up)).astype(
            jnp.bfloat16
        ),
        "head",
    ).astype(jnp.float32)
    unused_norm, pull_mlp = jax.vjp(rms_gain, hidden_state, gain_mlp)
    grad_norm_hidden, grad_gain_mlp = pull_mlp(grad_normed2)
    grad_hidden = grad_out + grad_norm_hidden
    grad_hidden_low = grad_hidden.astype(jnp.bfloat16)
    grad_w_out = contract_rows(mixed, grad_hidden_low)
    grad_mixed = contract_last(grad_hidden_low, w_out).astype(jnp.bfloat16)
    grad_seq = grad_mixed.reshape(head_shape)
    lse_seq = log_totals.reshape(seq_count, blocks, heads_here, BLOCK)

    def backward_sequence(sequence):
        query_all = lax.dynamic_index_in_dim(query_seq, sequence, 0, keepdims=False)
        key_all = lax.dynamic_index_in_dim(key_seq, sequence, 0, keepdims=False)
        value_all = lax.dynamic_index_in_dim(value_seq, sequence, 0, keepdims=False)
        grad_all = lax.dynamic_index_in_dim(grad_seq, sequence, 0, keepdims=False)
        lse_all = lax.dynamic_index_in_dim(lse_seq, sequence, 0, keepdims=False)

        def block_step(running, block_index):
            grad_key_acc, grad_value_acc = running
            first_row = block_index * BLOCK
            query_block = lax.dynamic_slice_in_dim(query_all, first_row, BLOCK, 0)
            grad_block = lax.dynamic_slice_in_dim(grad_all, first_row, BLOCK, 0)
            lse_block = lax.dynamic_index_in_dim(lse_all, block_index, 0, keepdims=False)
            scores = masked_scores(query_block, key_all, first_row, score_scale)
            probs = jnp.exp(scores - lse_block[..., None])
            grad_probs = jnp.einsum(
                "qhe,khe->hqk", grad_block, value_all, preferred_element_type=jnp.float32
            )
            inner_sum = jnp.sum(grad_probs * probs, axis=-1, keepdims=True)
            grad_scores = (probs * (grad_probs - inner_sum) * score_scale).astype(jnp.bfloat16)
            grad_value_acc = grad_value_acc + jnp.einsum(
                "hqk,qhe->khe",
                probs.astype(jnp.bfloat16),
                grad_block,
                preferred_element_type=jnp.float32,
            )
            grad_key_acc = grad_key_acc + jnp.einsum(
                "hqk,qhe->khe", grad_scores, query_block, preferred_element_type=jnp.float32
            )
            grad_query = jnp.einsum(
                "hqk,khe->qhe", grad_scores, key_all, preferred_element_type=jnp.float32
            )
            return ((grad_key_acc, grad_value_acc), grad_query.astype(jnp.bfloat16))

        empty_acc = jnp.zeros((length, heads_here, HD), jnp.float32)
        finals, grad_query_blocks = lax.scan(
            block_step, (empty_acc, empty_acc), jnp.arange(blocks, dtype=jnp.int32)
        )
        grad_key_seq = finals[0].astype(jnp.bfloat16).reshape(length, local_cols)
        grad_value_seq = finals[1].astype(jnp.bfloat16).reshape(length, local_cols)
        return (grad_query_blocks.reshape(length, local_cols), grad_key_seq, grad_value_seq)

    grad_q_all, grad_k_all, grad_v_all = lax.map(
        backward_sequence, jnp.arange(seq_count, dtype=jnp.int32)
    )
    grad_queries = grad_q_all.reshape(seq_count * length, local_cols)
    grad_keys = grad_k_all.reshape(seq_count * length, local_cols)
    grad_values = grad_v_all.reshape(seq_count * length, local_cols)
    grad_w_query = contract_rows(normed, grad_queries)
    grad_w_key = contract_rows(latent_state, grad_keys)
    grad_w_value = contract_rows(latent_state, grad_values)
    key_heads = w_key.reshape(latent_width, heads_here, HD)
    value_heads = w_value.reshape(latent_width, heads_here, HD)
    grad_latent = jnp.einsum(
        "lpe,cpe->lpc",
        grad_keys.reshape(-1, heads_here, HD),
        key_heads,
        preferred_element_type=jnp.float32,
    )
    grad_latent = grad_latent + jnp.einsum(
        "lpe,cpe->lpc",
        grad_values.reshape(-1, heads_here, HD),
        value_heads,
        preferred_element_type=jnp.float32,
    )
    grad_latent = grad_latent.astype(jnp.bfloat16)
    grad_w_lat = jnp.einsum("ld,lpc->dc", normed, grad_latent, preferred_element_type=jnp.float32)
    normed_part = contract_last(grad_queries, w_query) + jnp.einsum(
        "lpc,dc->ld", grad_latent, w_lat, preferred_element_type=jnp.float32
    )
    grad_normed = lax.psum(normed_part.astype(jnp.bfloat16), "head").astype(jnp.float32)
    unused_attn, pull_attn = jax.vjp(rms_gain, inputs, gain_attn)
    grad_norm_inputs, grad_gain_attn = pull_attn(grad_normed)
    grad_tokens = (grad_hidden + grad_norm_inputs).astype(jnp.bfloat16)
    half_rank = lax.axis_index("head") % half_size
    level_count = half_size.bit_length() - 1
    current = grad_w_lat
    for level in reversed(range(level_count)):
        width_half = current.shape[1] // 2
        lower_cols = current[:, :width_half]
        upper_cols = current[:, width_half:]
        upper_kept = half_rank >> level & 1 == 1
        kept_cols = jnp.where(upper_kept, upper_cols, lower_cols)
        given_cols = jnp.where(upper_kept, lower_cols, upper_cols)
        current = kept_cols + partner(given_cols.astype(jnp.bfloat16), "head", level).astype(
            given_cols.dtype
        )
    shards = (
        lax.psum_scatter(
            grad_gain_attn.astype(jnp.bfloat16), "dp", scatter_dimension=0, tiled=True
        ).astype(jnp.float32),
        lax.psum_scatter(
            grad_w_query.astype(jnp.bfloat16), "dp", scatter_dimension=0, tiled=True
        ).astype(jnp.float32),
        lax.psum_scatter(
            current.astype(jnp.bfloat16), "dp", scatter_dimension=0, tiled=True
        ).astype(jnp.float32),
        lax.psum_scatter(
            grad_w_key.astype(jnp.bfloat16), "dp", scatter_dimension=0, tiled=True
        ).astype(jnp.float32),
        lax.psum_scatter(
            grad_w_value.astype(jnp.bfloat16), "dp", scatter_dimension=0, tiled=True
        ).astype(jnp.float32),
        lax.psum_scatter(
            grad_w_out.astype(jnp.bfloat16), "dp", scatter_dimension=1, tiled=True
        ).astype(jnp.float32),
        lax.psum_scatter(
            grad_gain_mlp.astype(jnp.bfloat16), "dp", scatter_dimension=0, tiled=True
        ).astype(jnp.float32),
        lax.psum_scatter(
            grad_w_gate.astype(jnp.bfloat16), "dp", scatter_dimension=0, tiled=True
        ).astype(jnp.float32),
        lax.psum_scatter(
            grad_w_up.astype(jnp.bfloat16), "dp", scatter_dimension=0, tiled=True
        ).astype(jnp.float32),
        lax.psum_scatter(
            grad_w_down.astype(jnp.bfloat16), "dp", scatter_dimension=1, tiled=True
        ).astype(jnp.float32),
    )
    return (
        block_out,
        grad_tokens,
        shards[0],
        shards[1],
        shards[2],
        shards[3],
        shards[4],
        shards[5],
        shards[6],
        shards[7],
        shards[8],
        shards[9],
    )


def solution(mesh):
    in_specs = (
        P("dp", None),
        P("dp", None),
        P("dp"),
        P(),
        P(),
        P(None, "head"),
        P(),
        P(None, "head"),
        P(None, "head"),
        P("head", None),
        P(),
        P(None, "head"),
        P(None, "head"),
        P("head", None),
    )
    out_specs = (
        P("dp", None),
        P("dp", None),
        P("dp"),
        P("dp", "head"),
        P("dp", "head"),
        P("dp", "head"),
        P("dp", "head"),
        P("head", "dp"),
        P("dp"),
        P("dp", "head"),
        P("dp", "head"),
        P("head", "dp"),
    )
    return jax.shard_map(body, mesh=mesh, in_specs=in_specs, out_specs=out_specs, check_vma=False)
```

profile of v0, /device:TPU:0, one launch (start us, length us, event | category | flops | bytes accessed | tf_op | source)
XLA Modules:
  0.0 1046.1 jit_solution(8717948540972642519)
XLA Ops:
  7.3 3.2 fusion.96
  18.5 45.7 %while.40 = (s32[]{:T(128)}, bf16[4,512,128]{2,1,0:T(8,128)(2,1)S(1)}, f32[4,2,512]{2,1,0:T(2,128)S(1)}, s32[4]{0:T(128)S(1)}, bf16[1,2048,2,64]{1,3,2,0:T(8,128...) while((s32[]{:T(128)}, ...), condition=%wide.region_4.5_spmd, body=%wide.region_1.4_spmd.sunk | while | flops 563150336 | bytes 31232316 | solution.py:119
  33.2 2.9 fusion.194
  56.1 2.9 fusion.194
  64.3 3.3 convolution_convert_fusion.1
  69.3 157.4 %all-reduce.8.cloned.1.call-done = bf16[2048,1024]{1,0:T(8,128)(2,1)} async-done(((bf16[2048,1024]{1,0:T(8,128)(2,1)}), bf16[2048,1024]{1,0:T(8,128)(2,1)}) %all-reduce.8.cloned.1.call-update) | async-done | bytes 4194320 | tf_op jit(solution)/shard_map/psum | solution.py:123
  226.7 5.0 multiply_reduce_fusion.1
  238.2 4.8 multiply_convert_fusion.2
  246.5 4.6 add_convert_fusion.1
  251.4 5.2 convolution_convert_fusion.7
  256.6 5.2 convolution_convert_fusion.8
  262.2 5.9 convolution_convert_fusion
  268.1 3.2 fusion.110
  271.4 135.2 %all-reduce.10.cloned.1.call-done = bf16[2048,1024]{1,0:T(8,128)(2,1)} async-done(((bf16[2048,1024]{1,0:T(8,128)(2,1)}), bf16[2048,1024]{1,0:T(8,128)(2,1)}) %all-reduce.10.cloned.1.call-update) | async-done | bytes 4194320 | tf_op jit(solution)/shard_map/psum | solution.py:149
  406.6 7.7 fusion.91
  415.1 6.0 fusion.93
  421.1 3.2 copy-done.4
  426.6 189.0 %while.41 = (s32[]{:T(128)}, f32[2048,2,64]{0,2,1:T(8,128)}, f32[2048,2,64]{0,2,1:T(8,128)}, bf16[4,512,2,64]{1,3,2,0:T(8,128)(2,1)}, s32[4]{0:T(128)S(1)}, /*in...) while((s32[]{:T(128)}, f32[2048,2,64]{0,2,1:T(8,128)}, ...), condition=%wide.region_13.14_spmd.clone, body=%wide.region_11.13_spmd.clone.sunk | while | flops 1398872576 | bytes 149062032 | solution.py:199
  432.9 3.2 copy-done.3
  439.8 4.5 fusion.207
  444.3 14.3 %fusion.211 = bf16[4,512,2,64]{1,3,2,0:T(8,128)(2,1)} fusion(bf16[4,512,2,64]{1,3,2,0:T(8,128)(2,1)} %get-tuple-element.438, s32[]{:T(128)S(6)} %copy.59, bf16[2048,2,64]{0,2,1:T(8,128)(2,1)S(1)} %get-tuple-element.456, f32[2,512,2048]{2,1,0:T(8,128)} %fusion.207, f32[2,512,2048]{2,1,0:T(8,128)} %copy-done.3, ...), kind=kOutput, calls=%fused_computation.44.clone.1 | convolution fusion | flops 291572736 | bytes 36315140 | tf_op jit(solution)/shard_map/while/body/eval_jaxpr/while/body/eval_jaxpr/hqk,khe->qhe/dot_general | solution.py:193
  458.6 15.5 %fusion.209 = f32[2048,2,64]{0,2,1:T(8,128)} fusion(f32[2,512,2048]{2,1,0:T(8,128)} %fusion.207, f32[2,512,2048]{2,1,0:T(8,128)} %copy-done.3, f32[2,512]{1,0:T(2,128)S(1)} %dynamic-slice_bitcast_fusion.2, pred[512,2048]{1,0:T(8,128)(4,1)S(1)} %iota_compare_fusion.5, f32[2048,2,64]{0,2,1:T(8,128)} %get-tuple-element.436, pred[]{:T(512)S(6)} %compare.9, ...), kind=kOutput, calls=%fused_computation.41.clone.1 | convolution fusion | flops 292031488 | bytes 37888004 | tf_op jit(solution)/shard_map/while/body/eval_jaxpr/while/body/eval_jaxpr/hqk,qhe->khe/dot_general | solution.py:190
  480.3 3.2 copy-done.3
  487.1 4.5 fusion.207
  491.7 14.2 %fusion.211 = bf16[4,512,2,64]{1,3,2,0:T(8,128)(2,1)} fusion(bf16[4,512,2,64]{1,3,2,0:T(8,128)(2,1)} %get-tuple-element.438, s32[]{:T(128)S(6)} %copy.59, bf16[2048,2,64]{0,2,1:T(8,128)(2,1)S(1)} %get-tuple-element.456, f32[2,512,2048]{2,1,0:T(8,128)} %fusion.207, f32[2,512,2048]{2,1,0:T(8,128)} %copy-done.3, ...), kind=kOutput, calls=%fused_computation.44.clone.1 | convolution fusion | flops 291572736 | bytes 36315140 | tf_op jit(solution)/shard_map/while/body/eval_jaxpr/while/body/eval_jaxpr/hqk,khe->qhe/dot_general | solution.py:193
  505.8 15.4 %fusion.209 = f32[2048,2,64]{0,2,1:T(8,128)} fusion(f32[2,512,2048]{2,1,0:T(8,128)} %fusion.207, f32[2,512,2048]{2,1,0:T(8,128)} %copy-done.3, f32[2,512]{1,0:T(2,128)S(1)} %dynamic-slice_bitcast_fusion.2, pred[512,2048]{1,0:T(8,128)(4,1)S(1)} %iota_compare_fusion.5, f32[2048,2,64]{0,2,1:T(8,128)} %get-tuple-element.436, pred[]{:T(512)S(6)} %compare.9, ...), kind=kOutput, calls=%fused_computation.41.clone.1 | convolution fusion | flops 292031488 | bytes 37888004 | tf_op jit(solution)/shard_map/while/body/eval_jaxpr/while/body/eval_jaxpr/hqk,qhe->khe/dot_general | solution.py:190
  527.3 3.2 copy-done.3
  534.2 4.5 fusion.207
  538.7 14.1 %fusion.211 = bf16[4,512,2,64]{1,3,2,0:T(8,128)(2,1)} fusion(bf16[4,512,2,64]{1,3,2,0:T(8,128)(2,1)} %get-tuple-element.438, s32[]{:T(128)S(6)} %copy.59, bf16[2048,2,64]{0,2,1:T(8,128)(2,1)S(1)} %get-tuple-element.456, f32[2,512,2048]{2,1,0:T(8,128)} %fusion.207, f32[2,512,2048]{2,1,0:T(8,128)} %copy-done.3, ...), kind=kOutput, calls=%fused_computation.44.clone.1 | convolution fusion | flops 291572736 | bytes 36315140 | tf_op jit(solution)/shard_map/while/body/eval_jaxpr/while/body/eval_jaxpr/hqk,khe->qhe/dot_general | solution.py:193
  552.9 15.4 %fusion.209 = f32[2048,2,64]{0,2,1:T(8,128)} fusion(f32[2,512,2048]{2,1,0:T(8,128)} %fusion.207, f32[2,512,2048]{2,1,0:T(8,128)} %copy-done.3, f32[2,512]{1,0:T(2,128)S(1)} %dynamic-slice_bitcast_fusion.2, pred[512,2048]{1,0:T(8,128)(4,1)S(1)} %iota_compare_fusion.5, f32[2048,2,64]{0,2,1:T(8,128)} %get-tuple-element.436, pred[]{:T(512)S(6)} %compare.9, ...), kind=kOutput, calls=%fused_computation.41.clone.1 | convolution fusion | flops 292031488 | bytes 37888004 | tf_op jit(solution)/shard_map/while/body/eval_jaxpr/while/body/eval_jaxpr/hqk,qhe->khe/dot_general | solution.py:190
  574.4 3.2 copy-done.3
  581.3 4.5 fusion.207
  585.8 14.1 %fusion.211 = bf16[4,512,2,64]{1,3,2,0:T(8,128)(2,1)} fusion(bf16[4,512,2,64]{1,3,2,0:T(8,128)(2,1)} %get-tuple-element.438, s32[]{:T(128)S(6)} %copy.59, bf16[2048,2,64]{0,2,1:T(8,128)(2,1)S(1)} %get-tuple-element.456, f32[2,512,2048]{2,1,0:T(8,128)} %fusion.207, f32[2,512,2048]{2,1,0:T(8,128)} %copy-done.3, ...), kind=kOutput, calls=%fused_computation.44.clone.1 | convolution fusion | flops 291572736 | bytes 36315140 | tf_op jit(solution)/shard_map/while/body/eval_jaxpr/while/body/eval_jaxpr/hqk,khe->qhe/dot_general | solution.py:193
  599.9 15.4 %fusion.209 = f32[2048,2,64]{0,2,1:T(8,128)} fusion(f32[2,512,2048]{2,1,0:T(8,128)} %fusion.207, f32[2,512,2048]{2,1,0:T(8,128)} %copy-done.3, f32[2,512]{1,0:T(2,128)S(1)} %dynamic-slice_bitcast_fusion.2, pred[512,2048]{1,0:T(8,128)(4,1)S(1)} %iota_compare_fusion.5, f32[2048,2,64]{0,2,1:T(8,128)} %get-tuple-element.436, pred[]{:T(512)S(6)} %compare.9, ...), kind=kOutput, calls=%fused_computation.41.clone.1 | convolution fusion | flops 292031488 | bytes 37888004 | tf_op jit(solution)/shard_map/while/body/eval_jaxpr/while/body/eval_jaxpr/hqk,qhe->khe/dot_general | solution.py:190
  623.4 5.0 fusion.113
  629.7 3.0 convert_reduce_fusion
  632.7 4.5 fusion.128
  639.2 4.2 convolution_convert_fusion.9
  643.4 3.7 collective-permute-done
  650.1 4.5 fusion.126
  655.4 6.7 add_convert_fusion
  671.1 20.9 %reduce-scatter.17.cloned.1.call-done = bf16[128,256]{1,0:T(8,128)(2,1)} async-done(((bf16[128,1024]{1,0:T(8,128)(2,1)}), bf16[128,256]{1,0:T(8,128)(2,1)}) %reduce-scatter.17.cloned.1.call-update) | async-done | bytes 65552 | tf_op jit(solution)/shard_map/reduce_scatter | solution.py:267
  693.5 21.0 %reduce-scatter.9.cloned.1.call-done = bf16[256,128]{1,0:T(8,128)(2,1)} async-done(((bf16[1024,128]{1,0:T(8,128)(2,1)}), bf16[256,128]{1,0:T(8,128)(2,1)}) %reduce-scatter.9.cloned.1.call-update) | async-done | bytes 65552 | tf_op jit(solution)/shard_map/reduce_scatter | solution.py:255
  716.1 20.5 %reduce-scatter.11.cloned.1.call-done = bf16[256,64]{0,1:T(8,128)(2,1)} async-done(((bf16[1024,64]{0,1:T(8,128)(2,1)}), bf16[256,64]{0,1:T(8,128)(2,1)}) %reduce-scatter.11.cloned.1.call-update) | async-done | bytes 32784 | tf_op jit(solution)/shard_map/reduce_scatter | solution.py:258
  738.0 274.4 %all-reduce.12.cloned.1.call-done = (bf16[2048,1024]{1,0:T(8,128)(2,1)}, bf16[2048,1024]{1,0:T(8,128)(2,1)}) async-done(((bf16[2048,1024]{1,0:T(8,128)(2,1)}, bf16[2048,1024]{1,0:T(8,128)(2,1)}), (bf16[2048,1024]{1,0:T(8,128)(2,1)}, bf16[2048,1024]{1,0:T(8,128)(2,1)})) %all-reduce.12.cloned.1.call-update) | async-done | bytes 8388624 | tf_op jit(solution)/shard_map/psum | solution.py:129
  1012.4 5.6 fusion.92
  1018.0 6.9 all-reduce.3
  1025.5 13.6 %fusion.95 = (bf16[2048,1024]{1,0:T(8,128)(2,1)}, bf16[2048,1024]{1,0:T(8,128)(2,1)}) fusion(f32[2048,1024]{1,0:T(8,128)} %copy-done.4, bf16[2048,1024]{1,0:T(8,128)(2,1)} %get-tuple-element.261, bf16[2048,1024]{1,0:T(8,128)(2,1)} %param.18, f32[2048]{0:T(1024)S(1)} %multiply_multiply_fusion, f32[1024]{0:T(1024)S(1)} %copy-done.33, f32[2048]{0:T(1024)S(1)} %copy-done.29, ...), kind=kLoop, calls=%fused_computation.86 | loop fusion | flops 29360128 | bytes 33574912 | tf_op jit(solution)/shard_map/convert_element_type | solution.py:237
  (228 shorter events, 110.9 us)
Async XLA Ops:
  7.2 8.5 copy-start
  7.2 6.1 copy-start.21
  7.2 219.5 %all-reduce.8.cloned.1.call-start = ((), (), s32[]{:S(2)}) async-start(), calls=%async_computation.8 | async-start | bytes 8388608 | tf_op jit(solution)/shard_map/psum | solution.py:123
  10.5 6.5 copy-start.30
  10.5 6.5 copy-start.28
  13.3 3.7 copy-start.7
  13.3 4.7 copy-start.26
  18.5 45.8 %copy-start.18 = (bf16[128,1024]{1,0:T(8,128)(2,1)S(1)}, bf16[128,1024]{1,0:T(8,128)(2,1)}, u32[]{:S(2)}) copy-start(bf16[128,1024]{1,0:T(8,128)(2,1)} %param.27) | copy-start | bytes 786436
  64.3 167.5 %copy-start.11 = (bf16[4,512,128]{2,1,0:T(8,128)(2,1)}, bf16[4,512,128]{2,1,0:T(8,128)(2,1)S(1)}, u32[]{:S(2)}) copy-start(bf16[4,512,128]{2,1,0:T(8,128)(2,1)S(1)} %get-tuple-element.184) | copy-start | bytes 1572868
  64.3 4.5 copy-start.35
  67.5 164.3 %copy-start.32 = (f32[1024]{0:T(1024)S(1)}, f32[1024]{0:T(1024)}, u32[]{:S(2)}) copy-start(f32[1024]{0:T(1024)} %param.28) | copy-start | bytes 12292
  67.6 339.1 %all-reduce.10.cloned.1.call-start = ((), (), s32[]{:S(2)}) async-start(), calls=%async_computation.9 | async-start | bytes 8388608 | tf_op jit(solution)/shard_map/psum | solution.py:149
  226.7 5.1 copy-start.1
  226.7 5.9 copy-start.5
  232.7 3.7 copy-start.24
  234.3 3.8 copy-start.13
  234.3 3.9 copy-start.34
  251.1 412.3 %reduce-scatter.21.cloned.1.call-start = ((), (), s32[]{:S(2)}) async-start(), calls=%async_computation.16 | async-start | bytes 901120 | tf_op jit(solution)/shard_map/reduce_scatter | solution.py:276
  256.6 408.5 %reduce-scatter.19.cloned.1.call-start = ((), (), s32[]{:S(2)}) async-start(), calls=%async_computation.15 | async-start | bytes 901120 | tf_op jit(solution)/shard_map/reduce_scatter | solution.py:273
  261.8 405.0 %reduce-scatter.23.cloned.1.call-start = ((), (), s32[]{:S(2)}) async-start(), calls=%async_computation.17 | async-start | bytes 901120 | tf_op jit(solution)/shard_map/reduce_scatter | solution.py:279
  262.1 5.9 copy-start.14
  262.2 5.9 copy-start.37
  271.3 397.1 %reduce-scatter.13.cloned.1.call-start = ((), (), s32[]{:S(2)}) async-start(), calls=%async_computation.12 | async-start | bytes 81920 | tf_op jit(solution)/shard_map/reduce_scatter | solution.py:261
  406.6 7.8 copy-start.2
  406.6 7.8 copy-start.6
  406.6 8.4 copy-start.8
  430.0 6.1 copy-start.15
  430.0 6.1 copy-start.19
  477.3 6.1 copy-start.15
  477.3 6.1 copy-start.19
  524.4 6.1 copy-start.15
  524.4 6.1 copy-start.19
  571.5 6.1 copy-start.15
  571.5 6.1 copy-start.19
  616.9 11.6 %copy-start.10 = (bf16[2048,256]{1,0:T(8,128)(2,1)S(1)}, bf16[2048,256]{1,0:T(8,128)(2,1)}, u32[]{:S(2)}) copy-start(bf16[2048,256]{1,0:T(8,128)(2,1)} %copy-done.9) | copy-start | bytes 3145732
  628.4 8.9 copy-start.25
  628.4 41.4 %reduce-scatter.15.cloned.1.call-start = ((), (), s32[]{:S(2)}) async-start(), calls=%async_computation.13 | async-start | bytes 81920 | tf_op jit(solution)/shard_map/reduce_scatter | solution.py:264
  629.6 62.4 %reduce-scatter.17.cloned.1.call-start = ((), (), s32[]{:S(2)}) async-start(), calls=%async_computation.14 | async-start | bytes 327680 | tf_op jit(solution)/shard_map/reduce_scatter | solution.py:267
  632.7 17.3 %copy-start.22 = (bf16[1024,128]{1,0:T(8,128)(2,1)S(1)}, bf16[1024,128]{1,0:T(8,128)(2,1)}, u32[]{:S(2)}) copy-start(bf16[1024,128]{1,0:T(8,128)(2,1)} %param.23) | copy-start | bytes 786436
  637.8 76.8 %reduce-scatter.9.cloned.1.call-start = ((), (), s32[]{:S(2)}) async-start(), calls=%async_computation.10 | async-start | bytes 327680 | tf_op jit(solution)/shard_map/reduce_scatter | solution.py:255
  639.1 8.1 collective-permute-start
  643.4 93.2 %reduce-scatter.11.cloned.1.call-start = ((), (), s32[]{:S(2)}) async-start(), calls=%async_computation.11 | async-start | bytes 163840 | tf_op jit(solution)/shard_map/reduce_scatter | solution.py:258
  648.5 6.1 collective-permute-start.1
  655.3 6.8 copy-start.36
  655.3 357.1 %all-reduce.12.cloned.1.call-start = ((), (), s32[]{:S(2)}) async-start(), calls=%async_computation.18 | async-start | bytes 16777216 | tf_op jit(solution)/shard_map/psum | solution.py:129
  662.1 350.3 %copy-start.29 = (f32[2048]{0:T(1024)S(1)}, f32[2048]{0:T(1024)}, u32[]{:S(2)}) copy-start(f32[2048]{0:T(1024)} %copy-done.28) | copy-start | bytes 24580
  662.1 350.3 %copy-start.33 = (f32[1024]{0:T(1024)S(1)}, f32[1024]{0:T(1024)}, u32[]{:S(2)}) copy-start(f32[1024]{0:T(1024)} %param.22) | copy-start | bytes 12292
  662.1 355.9 %copy-start.31 = (f32[2048]{0:T(1024)S(1)}, f32[2048]{0:T(1024)}, u32[]{:S(2)}) copy-start(f32[2048]{0:T(1024)} %copy-done.30) | copy-start | bytes 24580
  (15 other events, 34.0 us)
Sparse Core Ops, SparseCore 0:
  67.7 159.0 all-reduce.7
  251.3 155.3 all-reduce.9
  409.2 21.8 reduce-scatter.20
  433.6 22.8 reduce-scatter.18
  458.9 22.8 reduce-scatter.22
  628.5 18.3 reduce-scatter.12
  649.9 19.4 reduce-scatter.14
  672.0 20.0 reduce-scatter.16
  694.5 20.0 reduce-scatter.8
  717.0 19.5 reduce-scatter.10
  741.3 271.0 all-reduce.11
where the time goes:
time: 1060 us; the launch traced here: 1050 us
  waiting for transfers between devices  633 us (60%)
  matrix products  257 us (24%)
  other arithmetic  80.2 us (8%)
  local copies, waits for them, and re-layouts  30.3 us (3%)
  loops' own time  19.2 us (2%)
  between operations  16.3 us (2%)
    psum x1, waiting for transfers between devices, body(): lax.psum(product(activated, w_down).astype(jnp.bfloat16), 'head')  274 us
    psum x1, waiting for transfers between devices, body(): lax.psum(product(mixed, w_out).astype(jnp.bfloat16), 'head')  157 us
    psum x1, waiting for transfers between devices, body(): lax.psum((contract_last(grad_gate, w_gate) + contract_last(up_projection_...  135 us
    dot_general x4, matrix products, block_step(): jnp.einsum('hqk,qhe->khe', grad_scores, query_block, preferred_element_ty...  61.8 us
    dot_general x4, matrix products, block_step(): jnp.einsum('hqk,khe->qhe', grad_scores, key_all, preferred_element_type=j...  56.8 us
    dot_general x7, matrix products, contract_rows(): lax.dot_general(left, right, (((0,), (0,)), ((), ())), preferred_element_...  26.2 us
  transfers between devices with their start and end apart: 13, of which 7 were waited for; matrix products, arithmetic and copies ran while one was open for 24% of the time, Pallas kernels for 0%

commit v1 on v0

v1 whole, which is shorter than its diff:
```python
import functools

import jax
import jax.numpy as jnp
from jax import lax
from jax.experimental import pallas as pl
from jax.experimental.pallas import tpu as pltpu
from jax.sharding import PartitionSpec as P

HD = 64
epsilon = 1e-05
negative = -1e30


def snake_order(count):
    return list(range(0, count, 2)) + list(range(count - 1, 0, -2))


class Ring:
    def __init__(self):
        self.count = lax.axis_size("head")
        order = snake_order(self.count)
        self.forward = [(order[i], order[(i + 1) % self.count]) for i in range(self.count)]
        self.backward = [(b, a) for a, b in self.forward]
        index = lax.axis_index("head")
        self.place = jnp.where(index % 2 == 0, index // 2, self.count - 1 - index // 2)

    def owner(self, offset):
        spot = (self.place + offset) % self.count
        half = self.count // 2
        return jnp.where(spot < half, 2 * spot, 2 * (self.count - 1 - spot) + 1)

    def gather(self, own):
        half = self.count // 2
        blocks = {0: own}
        ahead = behind = own
        for step in range(1, half):
            ahead = lax.ppermute(ahead, "head", self.forward)
            behind = lax.ppermute(behind, "head", self.backward)
            blocks[-step], blocks[step] = ahead, behind
        cut = own.shape[-1] // 2
        left = lax.ppermute(ahead[..., :cut], "head", self.forward)
        right = lax.ppermute(behind[..., cut:], "head", self.backward)
        blocks[half] = jnp.concatenate([left, right], axis=-1)
        return blocks

    def scatter(self, block):
        half = self.count // 2
        far = block(half)
        cut = far.shape[-1] // 2
        ahead = lax.ppermute(far[..., :cut], "head", self.forward)
        behind = lax.ppermute(far[..., cut:], "head", self.backward)
        for step in range(half - 1, 0, -1):
            give_ahead, give_behind = block(step), block(-step)
            if step == half - 1:
                give_ahead = jnp.concatenate(
                    [add(give_ahead[..., :cut], ahead), give_ahead[..., cut:]], axis=-1
                )
                give_behind = jnp.concatenate(
                    [give_behind[..., :cut], add(give_behind[..., cut:], behind)], axis=-1
                )
            else:
                give_ahead, give_behind = add(give_ahead, ahead), add(give_behind, behind)
            ahead = lax.ppermute(give_ahead, "head", self.forward)
            behind = lax.ppermute(give_behind, "head", self.backward)
        return wide(block(0)) + wide(ahead) + wide(behind)


def wide(block):
    return block.astype(jnp.float32)


def add(left, right):
    return (wide(left) + wide(right)).astype(jnp.bfloat16)


def flip(block, bit):
    count = lax.axis_size("dp")
    return lax.ppermute(block, "dp", [(i, i ^ bit) for i in range(count)])


def dp_gather(own):
    bits = lax.axis_size("dp").bit_length() - 1
    for bit in reversed(range(bits)):
        own = jnp.concatenate([own, flip(own, 1 << bit)], axis=0)
    return own


def dp_bit_order():
    bits = lax.axis_size("dp").bit_length() - 1
    order = [0]
    for bit in reversed(range(bits)):
        order = order + [r | 1 << bit for r in order]
    return order


def dp_scatter(blocks):
    bits = lax.axis_size("dp").bit_length() - 1
    for bit in range(bits):
        half = blocks.shape[0] // 2
        got = flip(blocks[half:], 1 << bit)
        if bit == bits - 1:
            return wide(blocks[:half]) + wide(got)
        blocks = add(blocks[:half], got)
    return wide(blocks)


def dot_last(a, b):
    return lax.dot_general(a, b, (((1,), (1,)), ((), ())), preferred_element_type=jnp.float32)

def dot_plain(a, b):
    return jnp.dot(a, b, preferred_element_type=jnp.float32)

def lane_heads(x, e):
    lane = lax.broadcasted_iota(jnp.int32, x.shape, 1)
    return jnp.where(lane // HD == e, x, jnp.zeros_like(x))

def segments(length, block):
    half = length // 2
    if block % 128 == 0:
        return ((0, half, 0, 2 * block, block), (half, length, block, 2 * block, block))
    return ((0, half, 0, 2 * block, 2 * block), (half, length, 0, 2 * block, 2 * block))

def visible(first_key, count, first_col, cols, block, rank, ranks):
    key = first_key + lax.broadcasted_iota(jnp.int32, (count, cols), 0)
    col = first_col + lax.broadcasted_iota(jnp.int32, (count, cols), 1)
    row = jnp.where(col < block, rank * block + col, (2 * ranks - 2 - rank) * block + col)
    return key <= row

def fwd_kernel(ranks, rank_ref, q_ref, k_ref, v_ref, o_ref, lse_ref):
    length = k_ref.shape[0]
    block = q_ref.shape[0] // 2
    rank = rank_ref[0]
    query = q_ref[...]
    value_t = v_ref[...].T
    outs, lses = [], []
    for e in range(q_ref.shape[1] // HD):
        query_e = lane_heads(query, e) * jnp.bfloat16(HD**-0.5)
        scores = []
        peak = jnp.full((1, 2 * block), negative, jnp.float32)
        for k0, k1, c0, c1, masked in segments(length, block):
            s = dot_last(k_ref[k0:k1, :], query_e[c0:c1, :])
            keep = visible(k0, k1 - k0, c0, masked, block, rank, ranks)
            if masked == c1 - c0:
                s = jnp.where(keep, s, negative)
            else:
                s = jnp.concatenate([jnp.where(keep, s[:, :masked], negative), s[:, masked:]], axis=1)
            top = jnp.max(s, axis=0, keepdims=True)
            if c0:
                top = jnp.concatenate([jnp.full((1, c0), negative, jnp.float32), top], axis=1)
            peak = jnp.maximum(peak, top)
            scores.append(s)
        total = jnp.zeros((1, 2 * block), jnp.float32)
        mixed = jnp.zeros((q_ref.shape[1], 2 * block), jnp.float32)
        for s, (k0, k1, c0, c1, masked) in zip(scores, segments(length, block)):
            w = jnp.exp(s - peak[:, c0:c1])
            part = jnp.sum(w, axis=0, keepdims=True)
            m = dot_plain(value_t[:, k0:k1], w.astype(jnp.bfloat16))
            if c0:
                part = jnp.concatenate([jnp.zeros((1, c0), jnp.float32), part], axis=1)
                m = jnp.concatenate([jnp.zeros((m.shape[0], c0), jnp.float32), m], axis=1)
            total += part
            mixed += m
        outs.append(mixed[e * HD:(e + 1) * HD] / total)
        lses.append(peak + jnp.log(total))
    o_ref[...] = jnp.concatenate(outs, axis=0).T.astype(o_ref.dtype)
    lse_ref[0] = jnp.concatenate(lses + [jnp.zeros((8 - len(lses), 2 * block), jnp.float32)], axis=0)

def attention_forward(rank, ranks, query, key, value):
    rows, width = query.shape
    length = key.shape[0]
    lanes = 2 * HD
    pairs = width // lanes
    return pl.pallas_call(
        functools.partial(fwd_kernel, ranks),
        grid=(pairs,),
        in_specs=[
            pl.BlockSpec(memory_space=pltpu.SMEM),
            pl.BlockSpec((rows, lanes), lambda i: (0, i)),
            pl.BlockSpec((length, lanes), lambda i: (0, i)),
            pl.BlockSpec((length, lanes), lambda i: (0, i)),
        ],
        out_specs=[
            pl.BlockSpec((rows, lanes), lambda i: (0, i)),
            pl.BlockSpec((1, 8, rows), lambda i: (i, 0, 0)),
        ],
        out_shape=[
            jax.ShapeDtypeStruct((rows, width), jnp.bfloat16),
            jax.ShapeDtypeStruct((pairs, 8, rows), jnp.float32),
        ],
        compiler_params=pltpu.CompilerParams(vmem_limit_bytes=48 * 2**20),
        cost_estimate=pl.CostEstimate(flops=4 * rows * length * width, bytes_accessed=4 * length * width, transcendentals=0),
        name="attention_forward",
    )(rank, query, key, value)

def bwd_kernel(ranks, step, rank_ref, q_ref, k_ref, v_ref, o_ref, g_ref, lse_ref, dq_ref, dk_ref, dv_ref):
    length = k_ref.shape[0]
    block = q_ref.shape[0] // 2
    rank = rank_ref[0]
    heads = q_ref.shape[1] // HD
    query, grad = q_ref[...], g_ref[...]
    key_t = k_ref[...].T
    spread = (grad.astype(jnp.float32) * o_ref[...].astype(jnp.float32)).T
    queries = [lane_heads(query, e) * jnp.bfloat16(HD**-0.5) for e in range(heads)]
    grads = [lane_heads(grad, e) for e in range(heads)]
    deltas = [jnp.sum(spread[e * HD:(e + 1) * HD], axis=0, keepdims=True) for e in range(heads)]
    dq = [jnp.zeros((q_ref.shape[1], 2 * block), jnp.float32) for e in range(heads)]
    for k0, k1, c0, c1, masked in segments(length, block):
        for s0 in range(k0, k1, step):
            k_c, v_c = k_ref[s0:s0 + step, :], v_ref[s0:s0 + step, :]
            keep = visible(s0, step, c0, masked, block, rank, ranks)
            dk = jnp.zeros((step, q_ref.shape[1]), jnp.float32)
            dv = jnp.zeros((step, q_ref.shape[1]), jnp.float32)
            for e in range(heads):
                s = dot_last(k_c, queries[e][c0:c1, :])
                p = jnp.exp(s - lse_ref[0, e:e + 1, c0:c1])
                if masked == c1 - c0:
                    p = jnp.where(keep, p, 0.0)
                else:
                    p = jnp.concatenate([jnp.where(keep, p[:, :masked], 0.0), p[:, masked:]], axis=1)
                dp = dot_last(v_c, grads[e][c0:c1, :])
                ds = (p * (dp - deltas[e][:, c0:c1])).astype(jnp.bfloat16)
                dv += dot_plain(p.astype(jnp.bfloat16), grads[e][c0:c1, :])
                dk += dot_plain(ds, queries[e][c0:c1, :])
                m = dot_plain(key_t[:, s0:s0 + step], ds)
                if c0:
                    m = jnp.concatenate([jnp.zeros((m.shape[0], c0), jnp.float32), m], axis=1)
                dq[e] += m
            dk_ref[s0:s0 + step, :] = dk.astype(jnp.bfloat16)
            dv_ref[s0:s0 + step, :] = dv.astype(jnp.bfloat16)
    own = jnp.concatenate([dq[e][e * HD:(e + 1) * HD] for e in range(heads)], axis=0)
    dq_ref[...] = (own * HD**-0.5).T.astype(jnp.bfloat16)

def attention_backward(rank, ranks, query, key, value, mixed, grad, lse, step=512):
    rows, width = query.shape
    length = key.shape[0]
    lanes = 2 * HD
    pairs = width // lanes
    row_spec = pl.BlockSpec((rows, lanes), lambda i: (0, i))
    key_spec = pl.BlockSpec((length, lanes), lambda i: (0, i))
    return pl.pallas_call(
        functools.partial(bwd_kernel, ranks, step),
        grid=(pairs,),
        in_specs=[
            pl.BlockSpec(memory_space=pltpu.SMEM),
            row_spec, key_spec, key_spec, row_spec, row_spec,
            pl.BlockSpec((1, 8, rows), lambda i: (i, 0, 0)),
        ],
        out_specs=[row_spec, key_spec, key_spec],
        out_shape=[
            jax.ShapeDtypeStruct((rows, width), jnp.bfloat16),
            jax.ShapeDtypeStruct((length, width), jnp.bfloat16),
            jax.ShapeDtypeStruct((length, width), jnp.bfloat16),
        ],
        compiler_params=pltpu.CompilerParams(vmem_limit_bytes=48 * 2**20),
        cost_estimate=pl.CostEstimate(flops=10 * rows * length * width, bytes_accessed=8 * length * width, transcendentals=0),
        name="attention_backward",
    )(rank, query, key, value, mixed, grad, lse)

def contract_rows(left, right):
    return lax.dot_general(
        left, right, (((0,), (0,)), ((), ())), preferred_element_type=jnp.float32
    )


def low(block):
    return block.astype(jnp.bfloat16)


def body(
    tokens,
    cotangent,
    group_ids,
    group_weights,
    gain_attn,
    w_query,
    w_latent,
    w_key,
    w_value,
    w_out,
    gain_mlp,
    w_gate,
    w_up,
    w_down,
):
    ring = Ring()
    ranks, members = ring.count, lax.axis_size("dp")
    rank, member = lax.axis_index("head"), lax.axis_index("dp")
    length, width = tokens.shape
    block = length // (2 * ranks)
    cols = w_query.shape[1]
    inner = w_key.shape[0]
    share = w_gate.shape[1] // members
    part = width // members
    order = dp_bit_order()

    def own_rows(whole, of=None):
        of = rank if of is None else of
        first = lax.dynamic_slice_in_dim(whole, of * block, block, 0)
        second = lax.dynamic_slice_in_dim(whole, (2 * ranks - 1 - of) * block, block, 0)
        return jnp.concatenate([first, second], axis=0)

    def place_rows(blocks):
        whole = jnp.zeros((length, blocks[0].shape[1]), blocks[0].dtype)
        for offset, piece in blocks.items():
            of = ring.owner(offset)
            whole = lax.dynamic_update_slice_in_dim(whole, piece[:block], of * block, 0)
            whole = lax.dynamic_update_slice_in_dim(
                whole, piece[block:], (2 * ranks - 1 - of) * block, 0
            )
        return whole

    packed = jnp.concatenate([w_query.T, w_key.T, w_value.T, w_out], axis=1)
    half_cols = cols // 2
    core = member % 2
    blocks = ring.gather(lax.dynamic_slice_in_dim(packed, core * half_cols, half_cols, 0))
    mine = jnp.zeros((ranks, half_cols, packed.shape[1]), packed.dtype)
    for offset, piece in blocks.items():
        mine = lax.dynamic_update_slice_in_dim(mine, piece[None], ring.owner(offset), 0)
    theirs = flip(mine, 1)
    first, second = jnp.where(core == 0, mine, theirs), jnp.where(core == 0, theirs, mine)
    packed = jnp.stack([first, second], axis=1).reshape(ranks * cols, packed.shape[1])
    query_t = packed[:, :width]
    key_t = packed[:, width : width + inner]
    value_t = packed[:, width + inner : width + 2 * inner]
    out_all = packed[:, width + 2 * inner :]

    gate_own = lax.dynamic_slice_in_dim(w_gate, member * share, share, 1).T
    up_own = lax.dynamic_slice_in_dim(w_up, member * share, share, 1).T
    down_own = lax.dynamic_slice_in_dim(w_down, member * share, share, 0)
    blocks = ring.gather(jnp.concatenate([gate_own, up_own, down_own], axis=0))
    offsets = list(blocks)
    gate_t = jnp.concatenate([blocks[o][:share] for o in offsets], axis=0)
    up_t = jnp.concatenate([blocks[o][share : 2 * share] for o in offsets], axis=0)
    down = jnp.concatenate([blocks[o][2 * share :] for o in offsets], axis=0)

    labels = jnp.arange(group_weights.shape[0], dtype=jnp.int32)
    row_weight = jnp.sum(jnp.where(group_ids[0] == labels, group_weights, 0.0))
    grad_out = wide(own_rows(cotangent)) * row_weight
    grad_low_all = dp_gather(low(grad_out))

    inputs = wide(tokens)
    root = lax.rsqrt(jnp.mean(inputs * inputs, axis=-1, keepdims=True) + epsilon)
    normed = low(inputs * root * gain_attn)
    latent = low(dot_plain(normed, w_latent))
    half_heads = query_t.shape[0] // 2
    latents = (latent[:, :inner], latent[:, inner:])

    def from_latents(weight_t):
        return jnp.concatenate(
            [
                low(dot_last(latents[0], weight_t[:half_heads])),
                low(dot_last(latents[1], weight_t[half_heads:])),
            ],
            axis=1,
        )

    keys, values = from_latents(key_t), from_latents(value_t)
    inputs_own, root_own, normed_own = own_rows(inputs), own_rows(root), own_rows(normed)
    queries = low(dot_last(normed_own, query_t))
    rank_ref = rank.astype(jnp.int32).reshape(1)
    mixed, lse = attention_forward(rank_ref, ranks, queries, keys, values)
    hidden = inputs_own + dot_plain(mixed, out_all)

    root_mlp = lax.rsqrt(jnp.mean(hidden * hidden, axis=-1, keepdims=True) + epsilon)
    normed_mlp = dp_gather(low(hidden * root_mlp * gain_mlp))
    gate = dot_last(normed_mlp, gate_t)
    up = dot_last(normed_mlp, up_t)
    logistic = jax.nn.sigmoid(gate)
    act = low(gate * logistic * up)
    grad_act = dot_last(grad_low_all, down)
    grad_gate = low(grad_act * up * logistic * (1.0 + gate * (1.0 - logistic)))
    grad_up = low(grad_act * gate * logistic)
    grad_normed_mlp = dp_scatter(low(dot_plain(grad_gate, gate_t) + dot_plain(grad_up, up_t)))
    mlp_out = dp_scatter(low(dot_plain(act, down)))
    block_out = place_rows(ring.gather(low(hidden + mlp_out)))

    grad_w_gate = low(contract_rows(grad_gate, normed_mlp))
    grad_w_up = low(contract_rows(grad_up, normed_mlp))
    grad_w_down = low(contract_rows(act, grad_low_all))

    def mlp_block(offset):
        spot = offsets.index(offset)
        rows = slice(spot * share, (spot + 1) * share)
        return jnp.concatenate([grad_w_gate[rows], grad_w_up[rows], grad_w_down[rows]], axis=0)

    mlp_grads = low(ring.scatter(mlp_block)).reshape(3, share, width)
    mlp_grads = wide(lax.all_to_all(mlp_grads, "dp", 2, 1, tiled=True))

    def norm_backward(incoming, gain, entered, scale):
        scaled = gain * incoming
        inner_mean = jnp.mean(scaled * entered, axis=-1, keepdims=True)
        grad = scale * scaled - entered * (scale * scale * scale) * inner_mean
        return grad, jnp.sum(incoming * entered * scale, axis=0)

    grad_hidden, grad_gain_mlp = norm_backward(grad_normed_mlp, gain_mlp, hidden, root_mlp)
    grad_hidden = grad_out + grad_hidden
    grad_hidden_low = low(grad_hidden)
    grad_mixed = low(dot_last(grad_hidden_low, out_all))

    def member_cols(whole, r):
        return lax.dynamic_slice_in_dim(whole, (member ^ order[r]) * part, part, 1)

    def by_member(left, right):
        return jnp.concatenate(
            [low(contract_rows(left, member_cols(right, r))) for r in range(members)], axis=0
        )

    grad_w_out = low(dp_scatter(by_member(mixed, grad_hidden_low)))

    grad_queries, grad_keys, grad_values = attention_backward(
        rank_ref, ranks, queries, keys, values, mixed, grad_mixed, lse
    )
    grad_latent = jnp.concatenate(
        [
            low(
                dot_plain(grad_keys[:, s], key_t[s]) + dot_plain(grad_values[:, s], value_t[s])
            )
            for s in (slice(0, half_heads), slice(half_heads, None))
        ],
        axis=1,
    )
    grad_latent_own = low(ring.scatter(lambda o: own_rows(grad_latent, ring.owner(o))))
    grad_normed = dot_plain(grad_queries, query_t) + dot_last(grad_latent_own, w_latent)
    grad_inputs, grad_gain_attn = norm_backward(grad_normed, gain_attn, inputs_own, root_own)
    grad_tokens = place_rows(ring.gather(low(grad_hidden + grad_inputs)))

    grad_w_query = by_member(grad_queries, normed_own)
    grad_w_latent = by_member(grad_latent_own, normed_own)
    rows_query = query_t.shape[0]
    rows_latent = w_latent.shape[1]
    joint = dp_scatter(
        jnp.concatenate(
            [
                grad_w_query.reshape(members, rows_query, part),
                grad_w_latent.reshape(members, rows_latent, part),
            ],
            axis=1,
        )
    )
    joint = low(joint[0])
    grad_w_kv = [
        jnp.concatenate(
            [
                low(contract_rows(latents[0], grad[:, :half_heads])),
                low(contract_rows(latents[1], grad[:, half_heads:])),
            ],
            axis=1,
        )
        for grad in (grad_keys, grad_values)
    ]
    inner_part = inner // members
    kv = low(
        dp_scatter(
            jnp.concatenate(
                [
                    lax.dynamic_slice_in_dim(g, (member ^ r) * inner_part, inner_part, 0)
                    for r in order
                    for g in grad_w_kv
                ],
                axis=0,
            )
        )
    )
    latent_cols = rows_latent // ranks

    def attn_block(offset):
        of = ring.owner(offset)
        kv_piece = lax.dynamic_slice_in_dim(kv, of * cols, cols, 1).reshape(-1, part)
        return jnp.concatenate(
            [
                lax.dynamic_slice_in_dim(grad_w_out, of * cols, cols, 0),
                lax.dynamic_slice_in_dim(joint, of * cols, cols, 0),
                lax.dynamic_slice_in_dim(joint, rows_query + of * latent_cols, latent_cols, 0),
                kv_piece,
            ],
            axis=0,
        )

    attn_grads = ring.scatter(attn_block)
    kv_grads = attn_grads[2 * cols + latent_cols :].reshape(2, inner_part, cols)

    gains = lax.psum(jnp.stack([grad_gain_attn, grad_gain_mlp]), ("head", "dp"))
    gains = lax.dynamic_slice_in_dim(gains, member * part, part, 1)
    return (
        block_out,
        grad_tokens,
        gains[0],
        attn_grads[cols : 2 * cols].T,
        attn_grads[2 * cols : 2 * cols + latent_cols].T,
        kv_grads[0],
        kv_grads[1],
        attn_grads[:cols],
        gains[1],
        mlp_grads[0].T,
        mlp_grads[1].T,
        mlp_grads[2],
    )


def solution(mesh):
    in_specs = (
        P("dp", None),
        P("dp", None),
        P("dp"),
        P(),
        P(),
        P(None, "head"),
        P(),
        P(None, "head"),
        P(None, "head"),
        P("head", None),
        P(),
        P(None, "head"),
        P(None, "head"),
        P("head", None),
    )
    out_specs = (
        P("dp", None),
        P("dp", None),
        P("dp"),
        P("dp", "head"),
        P("dp", "head"),
        P("dp", "head"),
        P("dp", "head"),
        P("head", "dp"),
        P("dp"),
        P("dp", "head"),
        P("dp", "head"),
        P("head", "dp"),
    )
    return jax.shard_map(body, mesh=mesh, in_specs=in_specs, out_specs=out_specs, check_vma=False)
```

time: 1060 us -> 466 us (0.44)
  waiting for transfers between devices: 633 us -> 113 us
  matrix products: 257 us -> 44.7 us
  starting transfers between devices: 2.74 us -> 72.5 us
  local copies, waits for them, and re-layouts: 30.3 us -> 86.1 us
  Pallas kernels: 0 us -> 41.4 us
  blocking collectives: 6.86 us -> 43.4 us
  other arithmetic: 80.2 us -> 54.1 us
  loops' own time: 19.2 us -> 0 us
  between operations: 16.3 us -> 3.33 us
    psum x3 -> x0, waiting for transfers between devices: 567 us -> none  [the longest x1 274 us: body(): lax.psum(product(activated, w_down).astype(jnp.bfloat16), 'head')]
    dot_general x45 -> x20, matrix products: 231 us -> 29.3 us  [the longest x10 14.7 us: dot_last(): lax.dot_general(a, b, (((1,), (1,)), ((), ())), preferred_element_type=jn...]
    ppermute x2 -> x71, waiting for transfers between devices: 3.72 us -> 113 us  [the longest x12 30.2 us: gather(): ahead = lax.ppermute(ahead, 'head', self.forward)]
    ppermute x2 -> x71, starting transfers between devices: 1.65 us -> 69 us  [the longest x12 18.2 us: gather(): ahead = lax.ppermute(ahead, 'head', self.forward)]
    reduce_scatter x8 -> x0, waiting for transfers between devices: 62.5 us -> none  [the longest x1 21 us: body(): lax.psum_scatter(grad_w_query.astype(jnp.bfloat16), 'dp', scatter_dimensi...]
    psum x0 -> x1, blocking collectives: none -> 43.4 us  [body(): gains = lax.psum(jnp.stack([grad_gain_attn, grad_gain_mlp]), ('head', 'dp'))]
    pallas_call x0 -> x2, Pallas kernels: none -> 41.3 us  [the longest x1 24.3 us: attention_backward(): pl.pallas_call(functools.partial(bwd_kernel, ranks, step), grid=(pairs,),...]
    dynamic_update_slice x8 -> x38, local copies, waits for them, and re-layouts: 0.56 us -> 37.5 us  [the longest x16 16.5 us: place_rows(): whole = lax.dynamic_update_slice_in_dim(whole, piece[:block], of * block, 0)]
  transfers between devices with their start and end apart: 13 -> 72, of which waited for: 7 -> 32; matrix products, arithmetic and copies ran while one was open for 24% -> 32% of each run, Pallas kernels for 0% -> 9%
where the time goes in v1:
time: 466 us; the launch traced here: 459 us
  waiting for transfers between devices  113 us (24%)
  local copies, waits for them, and re-layouts  86.1 us (18%)
  starting transfers between devices  72.5 us (16%)
  other arithmetic  54.1 us (12%)
  matrix products  44.7 us (10%)
  blocking collectives  43.4 us (9%)
  Pallas kernels  41.4 us (9%)
    psum x1, blocking collectives, body(): gains = lax.psum(jnp.stack([grad_gain_attn, grad_gain_mlp]), ('head', 'dp'))  43.4 us
    ppermute x12, waiting for transfers between devices, gather(): ahead = lax.ppermute(ahead, 'head', self.forward)  30.2 us
    ppermute x9, waiting for transfers between devices, scatter(): ahead = lax.ppermute(give_ahead, 'head', self.forward)  26.4 us
    pallas_call x1, Pallas kernels, attention_backward(): pl.pallas_call(functools.partial(bwd_kernel, ranks, step), grid=(pairs,),...  24.3 us
    ppermute x15, waiting for transfers between devices, flip(): return lax.ppermute(block, 'dp', [(i, i ^ bit) for i in range(count)])  22.5 us
    unnamed x127, local copies, waits for them, and re-layouts  19.8 us
    ppermute x12, starting transfers between devices, gather(): ahead = lax.ppermute(ahead, 'head', self.forward)  18.2 us
    pallas_call x1, Pallas kernels, attention_forward(): pl.pallas_call(functools.partial(fwd_kernel, ranks), grid=(pairs,), in_sp...  17 us
  transfers between devices with their start and end apart: 72, of which 32 were waited for; matrix products, arithmetic and copies ran while one was open for 32% of the time, Pallas kernels for 9%

profile of v1, /device:TPU:0, one launch (start us, length us, event | category | flops | bytes accessed | tf_op | source)
XLA Modules:
  0.0 458.8 jit_solution(18200720897556753124)
XLA Ops:
  6.3 3.0 collective-permute-start
  13.7 2.0 collective-permute-start.11
  16.4 3.1 multiply_reduce_fusion
  19.4 2.1 collective-permute-start.2
  23.0 12.5 %collective-permute-done.2 = bf16[64,2560]{1,0:T(8,128)(2,1)S(1)} collective-permute-done((bf16[64,2560]{1,0:T(8,128)(2,1)S(1)}, bf16[64,2560]{1,0:T(8,128)(2,1)S(1)}, u32[]{:S(2)}, u32[]{:S(2)}) %collective-permute-start.2) | collective-permute-done | bytes 327712 | tf_op jit(solution)/shard_map/ppermute | solution.py:38
  39.1 5.4 %collective-permute-done.4 = bf16[64,2560]{1,0:T(8,128)(2,1)S(1)} collective-permute-done((bf16[64,2560]{1,0:T(8,128)(2,1)S(1)}, bf16[64,2560]{1,0:T(8,128)(2,1)S(1)}, u32[]{:S(2)}, u32[]{:S(2)}) %collective-permute-start.4) | collective-permute-done | bytes 327712 | tf_op jit(solution)/shard_map/ppermute | solution.py:38
  54.1 2.0 copy-done.9
  59.6 3.4 convert_element_type.413
  63.1 2.4 convolution_convert_fusion.4
  67.6 4.9 %collective-permute-done.29 = bf16[256,1024]{1,0:T(8,128)(2,1)} collective-permute-done((bf16[256,1024]{1,0:T(8,128)(2,1)S(1)}, bf16[256,1024]{1,0:T(8,128)(2,1)}, u32[]{:S(2)}, u32[]{:S(2)}) %collective-permute-start.29) | collective-permute-done | bytes 524320 | tf_op jit(solution)/shard_map/ppermute | solution.py:79
  72.5 2.1 pad_maximum_fusion.9
  77.4 2.9 collective-permute-done.13
  82.5 2.9 select_bitcast_fusion.1
  89.6 2.7 pad_maximum_fusion.1
  92.3 17.0 %attention_forward.1 = (bf16[256,1024]{1,0:T(8,128)(2,1)S(1)}, f32[8,8,256]{2,1,0:T(8,128)S(1)}) custom-call(s32[1]{0:T(128)} %bitcast.rank_ref, bf16[256,1024]{1,0:T(8,128)(2,1)S(1)} %fusion.31.q_ref, bf16[2048,1024]{1,0:T(8,128)(2,1)S(1)} %get-tuple-element.209.k_ref, bf16[2048,1024]{1,0:T(8,128)(2,1)} %get-tuple-element.210.v_ref), custom_call_target="tpu_custom_call" | custom-call | flops 2147483648 | bytes 8388608 | tf_op jit(solution)/shard_map/attention_forward/pallas_call | solution.py:174
  118.6 4.6 collective-permute-done.9
  124.3 3.0 fusion.51
  129.0 5.0 %multiply_convert_fusion.2 = (bf16[1024,704]{0,1:T(8,128)(2,1)S(1)}, bf16[1024,704]{0,1:T(8,128)(2,1)S(1)}, bf16[1024,704]{0,1:T(8,128)(2,1)S(1)}) fusion(f32[1024,704]{0,1:T(8,128)S(1)} %fusion.51, f32[1024,704]{0,1:T(8,128)S(1)} %fusion.135, bf16[704,1024]{1,0:T(8,128)(2,1)S(1)} %get-tuple-element.147, bf16[512,1024]{1,0:T(8,128)(2,1)S(1)} %collective-permute-done.10, ...), kind=kOutput, calls=%fused_computation.47 | convolution fusion | flops 1494220800 | bytes 13631488 | tf_op jit(solution)/shard_map/dot_general | solution.py:109
  143.0 3.8 convolution_convert_fusion.6
  151.2 1.9 add_convert_fusion
  160.4 10.0 %collective-permute-done.64 = bf16[264,1024]{1,0:T(8,128)(2,1)} collective-permute-done((bf16[264,1024]{1,0:T(8,128)(2,1)}, bf16[264,1024]{1,0:T(8,128)(2,1)}, u32[]{:S(2)}, u32[]{:S(2)}) %collective-permute-start.64) | collective-permute-done | bytes 540704 | tf_op jit(solution)/shard_map/ppermute | solution.py:64
  181.1 2.8 collective-permute-done.65
  188.3 3.8 collective-permute-done.32
  192.6 7.1 %collective-permute-done.20 = bf16[256,1024]{1,0:T(8,128)(2,1)S(1)} collective-permute-done((bf16[256,1024]{1,0:T(8,128)(2,1)S(1)}, bf16[256,1024]{1,0:T(8,128)(2,1)S(1)}, u32[]{:S(2)}, u32[]{:S(2)}) %collective-permute-start.20) | collective-permute-done | bytes 524320 | tf_op jit(solution)/shard_map/ppermute | solution.py:79
  199.6 2.4 fusion.137
  204.3 24.3 %attention_backward.1 = (bf16[256,1024]{1,0:T(8,128)(2,1)S(1)}, bf16[2048,1024]{1,0:T(8,128)(2,1)}, bf16[2048,1024]{1,0:T(8,128)(2,1)}) custom-call(s32[1]{0:T(128)} %bitcast.rank_ref, bf16[256,1024]{1,0:T(8,128)(2,1)S(1)} %fusion.31.q_ref, bf16[2048,1024]{1,0:T(8,128)(2,1)} %copy-done.1, bf16[2048,1024]{1,0:T(8,128)(2,1)} %get-tuple-element.210.v_ref, ...), custom_call_target="tpu_custom_call" | custom-call | flops 5368709120 | bytes 16777216 | tf_op jit(solution)/shard_map/attention_backward/pallas_call | solution.py:241
  255.0 3.7 collective-permute-done.37
  264.4 3.5 all-to-all-start
  288.8 2.0 fusion.139
  290.8 2.0 copy.54
  301.0 2.9 collective-permute-done.40
  306.7 2.7 multiply_reduce_fusion.2
  311.7 43.4 %psum.7 = f32[2,1024]{1,0:T(2,128)S(1)} all-reduce(f32[2,1024]{1,0:T(2,128)S(1)} %pad_maximum_fusion.32), channel_id=1, replica_groups=mesh['head'=8,'dp'=4] {'head','dp'}, use_global_device_ids=true, to_apply=%region_7.8 | all-reduce | flops 2048 | bytes 16384 | tf_op jit(solution)/shard_map/psum | solution.py:483
  355.1 2.5 broadcast.74.clone.1
  362.1 2.4 collective-permute-start.50
  371.2 2.0 collective-permute-start.26
  378.0 2.0 collective-permute-start.44
  380.2 2.6 collective-permute-done.25
  382.9 3.3 collective-permute-done.26
  386.2 2.1 collective-permute-start.28
  391.2 7.3 %collective-permute-done.27 = bf16[256,512]{1,0:T(8,128)(2,1)S(1)} collective-permute-done((bf16[256,512]{1,0:T(8,128)(2,1)S(1)}, bf16[256,512]{1,0:T(8,128)(2,1)S(1)}, u32[]{:S(2)}, u32[]{:S(2)}) %collective-permute-start.27) | collective-permute-done | bytes 262176 | tf_op jit(solution)/shard_map/ppermute | solution.py:42
  398.5 3.3 collective-permute-done.28
  409.3 6.8 %collective-permute-done.45 = bf16[256,1024]{1,0:T(8,128)(2,1)S(1)} collective-permute-done((bf16[256,1024]{1,0:T(8,128)(2,1)S(1)}, bf16[256,1024]{1,0:T(8,128)(2,1)S(1)}, u32[]{:S(2)}, u32[]{:S(2)}) %collective-permute-start.45) | collective-permute-done | bytes 524320 | tf_op jit(solution)/shard_map/ppermute | solution.py:38
  424.7 2.1 collective-permute-done.52
  429.4 3.5 collective-permute-done.55
  435.2 5.4 %collective-permute-done.56 = bf16[384,256]{1,0:T(8,128)(2,1)S(1)} collective-permute-done((bf16[384,256]{1,0:T(8,128)(2,1)S(1)}, bf16[384,256]{1,0:T(8,128)(2,1)S(1)}, u32[]{:S(2)}, u32[]{:S(2)}) %collective-permute-start.56) | collective-permute-done | bytes 196640 | tf_op jit(solution)/shard_map/ppermute | solution.py:64
  443.0 4.8 %collective-permute-done.57 = bf16[384,256]{1,0:T(8,128)(2,1)S(1)} collective-permute-done((bf16[384,256]{1,0:T(8,128)(2,1)S(1)}, bf16[384,256]{1,0:T(8,128)(2,1)S(1)}, u32[]{:S(2)}, u32[]{:S(2)}) %collective-permute-start.57) | collective-permute-done | bytes 196640 | tf_op jit(solution)/shard_map/ppermute | solution.py:64
  450.8 2.8 collective-permute-done.58
  (439 shorter events, 205.3 us)
Async XLA Ops:
  6.3 13.1 %collective-permute-start = (bf16[64,2560]{1,0:T(8,128)(2,1)S(1)}, bf16[64,2560]{1,0:T(8,128)(2,1)S(1)}, u32[]{:S(2)}, u32[]{:S(2)}) collective-permute-start(bf16[64,2560]{1,0:T(8,128)(2,1)S(1)} %get-tuple-element.71), channel_id=1, source_target_pairs={{0,8},{8,16},{16,24},{24,28},{28,20},{20,12},{12,4},{4,0},{1,9},{9... | collective-permute-start | bytes 983048 | tf_op jit(solution)/shard_map/ppermute | solution.py:38
  9.3 12.2 %collective-permute-start.1 = (bf16[64,2560]{1,0:T(8,128)(2,1)S(1)}, bf16[64,2560]{1,0:T(8,128)(2,1)S(1)}, u32[]{:S(2)}, u32[]{:S(2)}) collective-permute-start(bf16[64,2560]{1,0:T(8,128)(2,1)S(1)} %get-tuple-element.71), channel_id=1, source_target_pairs={{8,0},{16,8},{24,16},{28,24},{20,28},{12,20},{4,12},{0,4},{9,1},{1... | collective-permute-start | bytes 983048 | tf_op jit(solution)/shard_map/ppermute | solution.py:39
  13.7 51.8 %collective-permute-start.11 = (bf16[264,1024]{1,0:T(8,128)(2,1)}, bf16[264,1024]{1,0:T(8,128)(2,1)}, u32[]{:S(2)}, u32[]{:S(2)}) collective-permute-start(bf16[264,1024]{1,0:T(8,128)(2,1)} %pad_maximum_fusion.15), channel_id=1, source_target_pairs={{0,8},{8,16},{16,24},{24,28},{28,20},{20,12},{12,4},{4,0},{1,9},{9... | collective-permute-start | bytes 1622024 | tf_op jit(solution)/shard_map/ppermute | solution.py:38
  15.7 51.5 %collective-permute-start.12 = (bf16[264,1024]{1,0:T(8,128)(2,1)}, bf16[264,1024]{1,0:T(8,128)(2,1)S(1)}, u32[]{:S(2)}, u32[]{:S(2)}) collective-permute-start(bf16[264,1024]{1,0:T(8,128)(2,1)} %pad_maximum_fusion.15), channel_id=1, source_target_pairs={{8,0},{16,8},{24,16},{28,24},{20,28},{12,20},{4,12},{0,4},{9,1},{1... | collective-permute-start | bytes 1622024 | tf_op jit(solution)/shard_map/ppermute | solution.py:39
  19.4 16.1 %collective-permute-start.2 = (bf16[64,2560]{1,0:T(8,128)(2,1)S(1)}, bf16[64,2560]{1,0:T(8,128)(2,1)S(1)}, u32[]{:S(2)}, u32[]{:S(2)}) collective-permute-start(bf16[64,2560]{1,0:T(8,128)(2,1)S(1)} %collective-permute-done), channel_id=1, source_target_pairs={{0,8},{8,16},{16,24},{24,28},{28,20},{20,12},{12,4},{4,0},{1,9},{9... | collective-permute-start | bytes 983048 | tf_op jit(solution)/shard_map/ppermute | solution.py:38
  21.5 15.9 %collective-permute-start.3 = (bf16[64,2560]{1,0:T(8,128)(2,1)S(1)}, bf16[64,2560]{1,0:T(8,128)(2,1)S(1)}, u32[]{:S(2)}, u32[]{:S(2)}) collective-permute-start(bf16[64,2560]{1,0:T(8,128)(2,1)S(1)} %collective-permute-done.1), channel_id=1, source_target_pairs={{8,0},{16,8},{24,16},{28,24},{20,28},{12,20},{4,12},{0,4},{9,1},{1... | collective-permute-start | bytes 983048 | tf_op jit(solution)/shard_map/ppermute | solution.py:39
  52.4 30.1 %collective-permute-start.8 = (bf16[8,64,2560]{2,1,0:T(8,128)(2,1)}, bf16[8,64,2560]{2,1,0:T(8,128)(2,1)}, u32[]{:S(2)}, u32[]{:S(2)}) collective-permute-start(bf16[8,64,2560]{2,1,0:T(8,128)(2,1)} %fusion.65), channel_id=1, source_target_pairs={{0,1},{1,0},{2,3},{3,2},{4,5},{5,4},{6,7},{7,6},{8,9},{9,8},{10,11... | collective-permute-start | bytes 7864328 | tf_op jit(solution)/shard_map/ppermute | solution.py:79
  58.0 14.5 %collective-permute-start.29 = (bf16[256,1024]{1,0:T(8,128)(2,1)S(1)}, bf16[256,1024]{1,0:T(8,128)(2,1)}, u32[]{:S(2)}, u32[]{:S(2)}) collective-permute-start(bf16[256,1024]{1,0:T(8,128)(2,1)S(1)} %fusion.49), channel_id=1, source_target_pairs={{0,2},{1,3},{2,0},{3,1},{4,6},{5,7},{6,4},{7,5},{8,10},{9,11},{10,... | collective-permute-start | bytes 1572872 | tf_op jit(solution)/shard_map/ppermute | solution.py:79
  65.5 14.8 %collective-permute-start.13 = (bf16[264,1024]{1,0:T(8,128)(2,1)}, bf16[264,1024]{1,0:T(8,128)(2,1)}, u32[]{:S(2)}, u32[]{:S(2)}) collective-permute-start(bf16[264,1024]{1,0:T(8,128)(2,1)} %collective-permute-done.11), channel_id=1, source_target_pairs={{0,8},{8,16},{16,24},{24,28},{28,20},{20,12},{12,4},{4,0},{1,9},{9... | collective-permute-start | bytes 1622024 | tf_op jit(solution)/shard_map/ppermute | solution.py:38
  67.1 14.7 %collective-permute-start.14 = (bf16[264,1024]{1,0:T(8,128)(2,1)S(1)}, bf16[264,1024]{1,0:T(8,128)(2,1)}, u32[]{:S(2)}, u32[]{:S(2)}) collective-permute-start(bf16[264,1024]{1,0:T(8,128)(2,1)S(1)} %collective-permute-done.12), channel_id=1, source_target_pairs={{8,0},{16,8},{24,16},{28,24},{20,28},{12,20},{4,12},{0,4},{9,1},{1... | collective-permute-start | bytes 1622024 | tf_op jit(solution)/shard_map/ppermute | solution.py:39
  74.6 49.4 %collective-permute-start.30 = (bf16[512,1024]{1,0:T(8,128)(2,1)}, bf16[512,1024]{1,0:T(8,128)(2,1)}, u32[]{:S(2)}, u32[]{:S(2)}) collective-permute-start(bf16[512,1024]{1,0:T(8,128)(2,1)} %pad_maximum_fusion.9), channel_id=1, source_target_pairs={{0,1},{1,0},{2,3},{3,2},{4,5},{5,4},{6,7},{7,6},{8,9},{9,8},{10,11... | collective-permute-start | bytes 3145736 | tf_op jit(solution)/shard_map/ppermute | solution.py:79
  80.3 34.0 %collective-permute-start.15 = (bf16[264,1024]{1,0:T(8,128)(2,1)}, bf16[264,1024]{1,0:T(8,128)(2,1)}, u32[]{:S(2)}, u32[]{:S(2)}) collective-permute-start(bf16[264,1024]{1,0:T(8,128)(2,1)} %collective-permute-done.13), channel_id=1, source_target_pairs={{0,8},{8,16},{16,24},{24,28},{28,20},{20,12},{12,4},{4,0},{1,9},{9... | collective-permute-start | bytes 1622024 | tf_op jit(solution)/shard_map/ppermute | solution.py:38
  81.9 35.0 %collective-permute-start.16 = (bf16[264,1024]{1,0:T(8,128)(2,1)}, bf16[264,1024]{1,0:T(8,128)(2,1)S(1)}, u32[]{:S(2)}, u32[]{:S(2)}) collective-permute-start(bf16[264,1024]{1,0:T(8,128)(2,1)} %collective-permute-done.14), channel_id=1, source_target_pairs={{8,0},{16,8},{24,16},{28,24},{20,28},{12,20},{4,12},{0,4},{9,1},{1... | collective-permute-start | bytes 1622024 | tf_op jit(solution)/shard_map/ppermute | solution.py:39
  110.4 12.7 %collective-permute-start.9 = (bf16[256,1024]{1,0:T(8,128)(2,1)S(1)}, bf16[256,1024]{1,0:T(8,128)(2,1)S(1)}, u32[]{:S(2)}, u32[]{:S(2)}) collective-permute-start(bf16[256,1024]{1,0:T(8,128)(2,1)S(1)} %multiply_convert_fusion.4), channel_id=1, source_target_pairs={{0,2},{1,3},{2,0},{3,1},{4,6},{5,7},{6,4},{7,5},{8,10},{9,11},{10,... | collective-permute-start | bytes 1572872 | tf_op jit(solution)/shard_map/ppermute | solution.py:79
  151.2 26.5 %collective-permute-start.19 = (bf16[512,1024]{1,0:T(8,128)(2,1)}, bf16[512,1024]{1,0:T(8,128)(2,1)}, u32[]{:S(2)}, u32[]{:S(2)}) collective-permute-start(bf16[512,1024]{1,0:T(8,128)(2,1)} %slice.628), channel_id=1, source_target_pairs={{0,1},{1,0},{2,3},{3,2},{4,5},{5,4},{6,7},{7,6},{8,9},{9,8},{10,11... | collective-permute-start | bytes 3145736 | tf_op jit(solution)/shard_map/ppermute | solution.py:79
  154.2 21.1 %collective-permute-start.31 = (bf16[512,1024]{1,0:T(8,128)(2,1)}, bf16[512,1024]{1,0:T(8,128)(2,1)}, u32[]{:S(2)}, u32[]{:S(2)}) collective-permute-start(bf16[512,1024]{1,0:T(8,128)(2,1)} %slice.650), channel_id=1, source_target_pairs={{0,1},{1,0},{2,3},{3,2},{4,5},{5,4},{6,7},{7,6},{8,9},{9,8},{10,11... | collective-permute-start | bytes 3145736 | tf_op jit(solution)/shard_map/ppermute | solution.py:79
  157.0 13.4 %collective-permute-start.64 = (bf16[264,1024]{1,0:T(8,128)(2,1)}, bf16[264,1024]{1,0:T(8,128)(2,1)}, u32[]{:S(2)}, u32[]{:S(2)}) collective-permute-start(bf16[264,1024]{1,0:T(8,128)(2,1)} %pad_maximum_fusion.18), channel_id=1, source_target_pairs={{0,8},{8,16},{16,24},{24,28},{28,20},{20,12},{12,4},{4,0},{1,9},{9... | collective-permute-start | bytes 1622024 | tf_op jit(solution)/shard_map/ppermute | solution.py:64
  159.5 13.8 %collective-permute-start.68 = (bf16[264,1024]{1,0:T(8,128)(2,1)}, bf16[264,1024]{1,0:T(8,128)(2,1)}, u32[]{:S(2)}, u32[]{:S(2)}) collective-permute-start(bf16[264,1024]{1,0:T(8,128)(2,1)} %pad_maximum_fusion.20), channel_id=1, source_target_pairs={{8,0},{16,8},{24,16},{28,24},{20,28},{12,20},{4,12},{0,4},{9,1},{1... | collective-permute-start | bytes 1622024 | tf_op jit(solution)/shard_map/ppermute | solution.py:65
  171.7 12.2 %collective-permute-start.65 = (bf16[264,1024]{1,0:T(8,128)(2,1)S(1)}, bf16[264,1024]{1,0:T(8,128)(2,1)S(1)}, u32[]{:S(2)}, u32[]{:S(2)}) collective-permute-start(bf16[264,1024]{1,0:T(8,128)(2,1)S(1)} %add_convert_fusion.10), channel_id=1, source_target_pairs={{0,8},{8,16},{16,24},{24,28},{28,20},{20,12},{12,4},{4,0},{1,9},{9... | collective-permute-start | bytes 1622024 | tf_op jit(solution)/shard_map/ppermute | solution.py:64
  174.8 11.9 %collective-permute-start.69 = (bf16[264,1024]{1,0:T(8,128)(2,1)S(1)}, bf16[264,1024]{1,0:T(8,128)(2,1)S(1)}, u32[]{:S(2)}, u32[]{:S(2)}) collective-permute-start(bf16[264,1024]{1,0:T(8,128)(2,1)S(1)} %add_convert_fusion.8), channel_id=1, source_target_pairs={{8,0},{16,8},{24,16},{28,24},{20,28},{12,20},{4,12},{0,4},{9,1},{1... | collective-permute-start | bytes 1622024 | tf_op jit(solution)/shard_map/ppermute | solution.py:65
  177.1 14.9 %collective-permute-start.32 = (bf16[256,1024]{1,0:T(8,128)(2,1)S(1)}, bf16[256,1024]{1,0:T(8,128)(2,1)S(1)}, u32[]{:S(2)}, u32[]{:S(2)}) collective-permute-start(bf16[256,1024]{1,0:T(8,128)(2,1)S(1)} %slice.652), channel_id=1, source_target_pairs={{0,2},{1,3},{2,0},{3,1},{4,6},{5,7},{6,4},{7,5},{8,10},{9,11},{10,... | collective-permute-start | bytes 1572872 | tf_op jit(solution)/shard_map/ppermute | solution.py:79
  179.6 20.1 %collective-permute-start.20 = (bf16[256,1024]{1,0:T(8,128)(2,1)S(1)}, bf16[256,1024]{1,0:T(8,128)(2,1)S(1)}, u32[]{:S(2)}, u32[]{:S(2)}) collective-permute-start(bf16[256,1024]{1,0:T(8,128)(2,1)S(1)} %slice.630), channel_id=1, source_target_pairs={{0,2},{1,3},{2,0},{3,1},{4,6},{5,7},{6,4},{7,5},{8,10},{9,11},{10,... | collective-permute-start | bytes 1572872 | tf_op jit(solution)/shard_map/ppermute | solution.py:79
  184.9 74.6 %collective-permute-start.66 = (bf16[264,1024]{1,0:T(8,128)(2,1)}, bf16[264,1024]{1,0:T(8,128)(2,1)}, u32[]{:S(2)}, u32[]{:S(2)}) collective-permute-start(bf16[264,1024]{1,0:T(8,128)(2,1)} %add_convert_fusion.9), channel_id=1, source_target_pairs={{0,8},{8,16},{16,24},{24,28},{28,20},{20,12},{12,4},{4,0},{1,9},{9... | collective-permute-start | bytes 1622024 | tf_op jit(solution)/shard_map/ppermute | solution.py:64
  187.7 73.4 %collective-permute-start.70 = (bf16[264,1024]{1,0:T(8,128)(2,1)}, bf16[264,1024]{1,0:T(8,128)(2,1)}, u32[]{:S(2)}, u32[]{:S(2)}) collective-permute-start(bf16[264,1024]{1,0:T(8,128)(2,1)} %add_convert_fusion.7), channel_id=1, source_target_pairs={{8,0},{16,8},{24,16},{28,24},{20,28},{12,20},{4,12},{0,4},{9,1},{1... | collective-permute-start | bytes 1622024 | tf_op jit(solution)/shard_map/ppermute | solution.py:65
  238.1 37.2 %collective-permute-start.21 = (bf16[256,1024]{1,0:T(8,128)(2,1)}, bf16[256,1024]{1,0:T(8,128)(2,1)}, u32[]{:S(2)}, u32[]{:S(2)}) collective-permute-start(bf16[256,1024]{1,0:T(8,128)(2,1)} %get-tuple-element.126), channel_id=1, source_target_pairs={{0,8},{8,16},{16,24},{24,28},{28,20},{20,12},{12,4},{4,0},{1,9},{9... | collective-permute-start | bytes 1572872 | tf_op jit(solution)/shard_map/ppermute | solution.py:38
  239.7 40.3 %collective-permute-start.22 = (bf16[256,1024]{1,0:T(8,128)(2,1)}, bf16[256,1024]{1,0:T(8,128)(2,1)}, u32[]{:S(2)}, u32[]{:S(2)}) collective-permute-start(bf16[256,1024]{1,0:T(8,128)(2,1)} %get-tuple-element.126), channel_id=1, source_target_pairs={{8,0},{16,8},{24,16},{28,24},{20,28},{12,20},{4,12},{0,4},{9,1},{1... | collective-permute-start | bytes 1572872 | tf_op jit(solution)/shard_map/ppermute | solution.py:39
  258.7 13.7 %collective-permute-start.53 = (bf16[256,1024]{1,0:T(8,128)(2,1)}, bf16[256,1024]{1,0:T(8,128)(2,1)}, u32[]{:S(2)}, u32[]{:S(2)}) collective-permute-start(bf16[256,1024]{1,0:T(8,128)(2,1)} %pad_maximum_fusion.23), channel_id=1, source_target_pairs={{0,1},{1,0},{2,3},{3,2},{4,5},{5,4},{6,7},{7,6},{8,9},{9,8},{10,11... | collective-permute-start | bytes 1572872 | tf_op jit(solution)/shard_map/ppermute | solution.py:79
  264.4 24.2 %all-to-all-start = ((bf16[3,88,1024]{1,0,2:T(4,128)(2,1)}), bf16[3,88,1024]{1,0,2:T(4,128)(2,1)S(1)}, u32[]{:S(2)}, u32[]{:S(2)}) async-start(bf16[3,88,1024]{1,0,2:T(4,128)(2,1)} %copy.53), calls=%async_computation | async-start | bytes 2097152 | tf_op jit(solution)/shard_map/all_to_all | solution.py:388
  268.5 91.6 %collective-permute-start.49 = (bf16[2048,256]{1,0:T(8,128)(2,1)}, bf16[2048,256]{1,0:T(8,128)(2,1)}, u32[]{:S(2)}, u32[]{:S(2)}) collective-permute-start(bf16[2048,256]{1,0:T(8,128)(2,1)} %pad_maximum_fusion.10), channel_id=1, source_target_pairs={{0,1},{1,0},{2,3},{3,2},{4,5},{5,4},{6,7},{7,6},{8,9},{9,8},{10,11... | collective-permute-start | bytes 3145736 | tf_op jit(solution)/shard_map/ppermute | solution.py:79
  269.9 15.1 %collective-permute-start.35 = (bf16[256,512]{0,1:T(8,128)(2,1)S(1)}, bf16[256,512]{0,1:T(8,128)(2,1)S(1)}, u32[]{:S(2)}, u32[]{:S(2)}) collective-permute-start(bf16[256,512]{0,1:T(8,128)(2,1)S(1)} %add_convert_fusion.22), channel_id=1, source_target_pairs={{0,8},{8,16},{16,24},{24,28},{28,20},{20,12},{12,4},{4,0},{1,9},{9... | collective-permute-start | bytes 786440 | tf_op jit(solution)/shard_map/ppermute | solution.py:64
  272.5 13.8 %collective-permute-start.39 = (bf16[256,512]{0,1:T(8,128)(2,1)S(1)}, bf16[256,512]{0,1:T(8,128)(2,1)S(1)}, u32[]{:S(2)}, u32[]{:S(2)}) collective-permute-start(bf16[256,512]{0,1:T(8,128)(2,1)S(1)} %add_convert_fusion.20), channel_id=1, source_target_pairs={{8,0},{16,8},{24,16},{28,24},{20,28},{12,20},{4,12},{0,4},{9,1},{1... | collective-permute-start | bytes 786440 | tf_op jit(solution)/shard_map/ppermute | solution.py:65
  275.3 20.3 %collective-permute-start.54 = (bf16[128,1024]{1,0:T(8,128)(2,1)}, bf16[128,1024]{1,0:T(8,128)(2,1)}, u32[]{:S(2)}, u32[]{:S(2)}) collective-permute-start(bf16[128,1024]{1,0:T(8,128)(2,1)} %slice.684), channel_id=1, source_target_pairs={{0,2},{1,3},{2,0},{3,1},{4,6},{5,7},{6,4},{7,5},{8,10},{9,11},{10,... | collective-permute-start | bytes 786440 | tf_op jit(solution)/shard_map/ppermute | solution.py:79
  280.0 82.1 %collective-permute-start.23 = (bf16[256,1024]{1,0:T(8,128)(2,1)}, bf16[256,1024]{1,0:T(8,128)(2,1)}, u32[]{:S(2)}, u32[]{:S(2)}) collective-permute-start(bf16[256,1024]{1,0:T(8,128)(2,1)} %collective-permute-done.21), channel_id=1, source_target_pairs={{0,8},{8,16},{16,24},{24,28},{28,20},{20,12},{12,4},{4,0},{1,9},{9... | collective-permute-start | bytes 1572872 | tf_op jit(solution)/shard_map/ppermute | solution.py:38
  285.0 82.8 %collective-permute-start.24 = (bf16[256,1024]{1,0:T(8,128)(2,1)}, bf16[256,1024]{1,0:T(8,128)(2,1)}, u32[]{:S(2)}, u32[]{:S(2)}) collective-permute-start(bf16[256,1024]{1,0:T(8,128)(2,1)} %collective-permute-done.22), channel_id=1, source_target_pairs={{8,0},{16,8},{24,16},{28,24},{20,28},{12,20},{4,12},{0,4},{9,1},{1... | collective-permute-start | bytes 1572872 | tf_op jit(solution)/shard_map/ppermute | solution.py:39
  286.2 14.7 %collective-permute-start.36 = (bf16[256,512]{0,1:T(8,128)(2,1)}, bf16[256,512]{0,1:T(8,128)(2,1)}, u32[]{:S(2)}, u32[]{:S(2)}) collective-permute-start(bf16[256,512]{0,1:T(8,128)(2,1)} %add_convert_fusion.21), channel_id=1, source_target_pairs={{0,8},{8,16},{16,24},{24,28},{28,20},{20,12},{12,4},{4,0},{1,9},{9... | collective-permute-start | bytes 786440 | tf_op jit(solution)/shard_map/ppermute | solution.py:64
  309.6 61.5 %collective-permute-start.41 = (bf16[256,1024]{1,0:T(8,128)(2,1)S(1)}, bf16[256,1024]{1,0:T(8,128)(2,1)}, u32[]{:S(2)}, u32[]{:S(2)}) collective-permute-start(bf16[256,1024]{1,0:T(8,128)(2,1)S(1)} %add_convert_fusion.13), channel_id=1, source_target_pairs={{0,8},{8,16},{16,24},{24,28},{28,20},{20,12},{12,4},{4,0},{1,9},{9... | collective-permute-start | bytes 1572872 | tf_op jit(solution)/shard_map/ppermute | solution.py:38
  311.0 65.5 %collective-permute-start.42 = (bf16[256,1024]{1,0:T(8,128)(2,1)S(1)}, bf16[256,1024]{1,0:T(8,128)(2,1)S(1)}, u32[]{:S(2)}, u32[]{:S(2)}) collective-permute-start(bf16[256,1024]{1,0:T(8,128)(2,1)S(1)} %add_convert_fusion.13), channel_id=1, source_target_pairs={{8,0},{16,8},{24,16},{28,24},{20,28},{12,20},{4,12},{0,4},{9,1},{1... | collective-permute-start | bytes 1572872 | tf_op jit(solution)/shard_map/ppermute | solution.py:39
  360.1 48.4 %collective-permute-start.51 = (bf16[2,1536,256]{2,1,0:T(8,128)(2,1)S(1)}, bf16[2,1536,256]{2,1,0:T(8,128)(2,1)S(1)}, u32[]{:S(2)}, u32[]{:S(2)}) collective-permute-start(bf16[2,1536,256]{2,1,0:T(8,128)(2,1)S(1)} %pad_maximum_fusion.6), channel_id=1, source_target_pairs={{0,1},{1,0},{2,3},{3,2},{4,5},{5,4},{6,7},{7,6},{8,9},{9,8},{10,11... | collective-permute-start | bytes 4718600 | tf_op jit(solution)/shard_map/ppermute | solution.py:79
  362.1 15.9 %collective-permute-start.50 = (bf16[1024,256]{1,0:T(8,128)(2,1)S(1)}, bf16[1024,256]{1,0:T(8,128)(2,1)S(1)}, u32[]{:S(2)}, u32[]{:S(2)}) collective-permute-start(bf16[1024,256]{1,0:T(8,128)(2,1)S(1)} %slice.678), channel_id=1, source_target_pairs={{0,2},{1,3},{2,0},{3,1},{4,6},{5,7},{6,4},{7,5},{8,10},{9,11},{10,... | collective-permute-start | bytes 1572872 | tf_op jit(solution)/shard_map/ppermute | solution.py:79
  367.8 15.0 %collective-permute-start.25 = (bf16[256,1024]{1,0:T(8,128)(2,1)}, bf16[256,1024]{1,0:T(8,128)(2,1)S(1)}, u32[]{:S(2)}, u32[]{:S(2)}) collective-permute-start(bf16[256,1024]{1,0:T(8,128)(2,1)} %collective-permute-done.23), channel_id=1, source_target_pairs={{0,8},{8,16},{16,24},{24,28},{28,20},{20,12},{12,4},{4,0},{1,9},{9... | collective-permute-start | bytes 1572872 | tf_op jit(solution)/shard_map/ppermute | solution.py:38
  371.2 15.0 %collective-permute-start.26 = (bf16[256,1024]{1,0:T(8,128)(2,1)}, bf16[256,1024]{1,0:T(8,128)(2,1)S(1)}, u32[]{:S(2)}, u32[]{:S(2)}) collective-permute-start(bf16[256,1024]{1,0:T(8,128)(2,1)} %collective-permute-done.24), channel_id=1, source_target_pairs={{8,0},{16,8},{24,16},{28,24},{20,28},{12,20},{4,12},{0,4},{9,1},{1... | collective-permute-start | bytes 1572872 | tf_op jit(solution)/shard_map/ppermute | solution.py:39
  376.5 26.8 %collective-permute-start.43 = (bf16[256,1024]{1,0:T(8,128)(2,1)}, bf16[256,1024]{1,0:T(8,128)(2,1)S(1)}, u32[]{:S(2)}, u32[]{:S(2)}) collective-permute-start(bf16[256,1024]{1,0:T(8,128)(2,1)} %collective-permute-done.41), channel_id=1, source_target_pairs={{0,8},{8,16},{16,24},{24,28},{28,20},{20,12},{12,4},{4,0},{1,9},{9... | collective-permute-start | bytes 1572872 | tf_op jit(solution)/shard_map/ppermute | solution.py:38
  378.0 26.7 %collective-permute-start.44 = (bf16[256,1024]{1,0:T(8,128)(2,1)S(1)}, bf16[256,1024]{1,0:T(8,128)(2,1)S(1)}, u32[]{:S(2)}, u32[]{:S(2)}) collective-permute-start(bf16[256,1024]{1,0:T(8,128)(2,1)S(1)} %collective-permute-done.42), channel_id=1, source_target_pairs={{8,0},{16,8},{24,16},{28,24},{20,28},{12,20},{4,12},{0,4},{9,1},{1... | collective-permute-start | bytes 1572872 | tf_op jit(solution)/shard_map/ppermute | solution.py:39
  382.9 15.6 %collective-permute-start.27 = (bf16[256,512]{1,0:T(8,128)(2,1)S(1)}, bf16[256,512]{1,0:T(8,128)(2,1)S(1)}, u32[]{:S(2)}, u32[]{:S(2)}) collective-permute-start(bf16[256,512]{1,0:T(8,128)(2,1)S(1)} %slice.645), channel_id=1, source_target_pairs={{0,8},{8,16},{16,24},{24,28},{28,20},{20,12},{12,4},{4,0},{1,9},{9... | collective-permute-start | bytes 786440 | tf_op jit(solution)/shard_map/ppermute | solution.py:42
  386.2 15.6 %collective-permute-start.28 = (bf16[256,512]{1,0:T(8,128)(2,1)S(1)}, bf16[256,512]{1,0:T(8,128)(2,1)S(1)}, u32[]{:S(2)}, u32[]{:S(2)}) collective-permute-start(bf16[256,512]{1,0:T(8,128)(2,1)S(1)} %slice.646), channel_id=1, source_target_pairs={{8,0},{16,8},{24,16},{28,24},{20,28},{12,20},{4,12},{0,4},{9,1},{1... | collective-permute-start | bytes 786440 | tf_op jit(solution)/shard_map/ppermute | solution.py:43
  403.3 12.7 %collective-permute-start.45 = (bf16[256,1024]{1,0:T(8,128)(2,1)S(1)}, bf16[256,1024]{1,0:T(8,128)(2,1)S(1)}, u32[]{:S(2)}, u32[]{:S(2)}) collective-permute-start(bf16[256,1024]{1,0:T(8,128)(2,1)S(1)} %collective-permute-done.43), channel_id=1, source_target_pairs={{0,8},{8,16},{16,24},{24,28},{28,20},{20,12},{12,4},{4,0},{1,9},{9... | collective-permute-start | bytes 1572872 | tf_op jit(solution)/shard_map/ppermute | solution.py:38
  404.7 12.8 %collective-permute-start.46 = (bf16[256,1024]{1,0:T(8,128)(2,1)S(1)}, bf16[256,1024]{1,0:T(8,128)(2,1)S(1)}, u32[]{:S(2)}, u32[]{:S(2)}) collective-permute-start(bf16[256,1024]{1,0:T(8,128)(2,1)S(1)} %collective-permute-done.44), channel_id=1, source_target_pairs={{8,0},{16,8},{24,16},{28,24},{20,28},{12,20},{4,12},{0,4},{9,1},{1... | collective-permute-start | bytes 1572872 | tf_op jit(solution)/shard_map/ppermute | solution.py:39
  409.0 17.9 %collective-permute-start.52 = (bf16[1,1536,256]{2,1,0:T(8,128)(2,1)S(1)}, bf16[1,1536,256]{2,1,0:T(8,128)(2,1)S(1)}, u32[]{:S(2)}, u32[]{:S(2)}) collective-permute-start(bf16[1,1536,256]{2,1,0:T(8,128)(2,1)S(1)} %slice.682), channel_id=1, source_target_pairs={{0,2},{1,3},{2,0},{3,1},{4,6},{5,7},{6,4},{7,5},{8,10},{9,11},{10,... | collective-permute-start | bytes 2359304 | tf_op jit(solution)/shard_map/ppermute | solution.py:79
  (80 other events, 813.1 us)

commit v2 on v1

--- a/solution.py
+++ b/solution.py
@@ -16,54 +16,140 @@
     return list(range(0, count, 2)) + list(range(count - 1, 0, -2))
 
 
+def after(block, *earlier):
+    return lax.optimization_barrier((block, earlier))[0] if earlier else block
+
+
 class Ring:
     def __init__(self):
         self.count = lax.axis_size("head")
+        self.half = self.count // 2
         order = snake_order(self.count)
         self.forward = [(order[i], order[(i + 1) % self.count]) for i in range(self.count)]
         self.backward = [(b, a) for a, b in self.forward]
         index = lax.axis_index("head")
         self.place = jnp.where(index % 2 == 0, index // 2, self.count - 1 - index // 2)
+        self.offsets = [0]
+        for step in range(1, self.half):
+            self.offsets += [-step, step]
+        self.offsets.append(self.half)
 
     def owner(self, offset):
         spot = (self.place + offset) % self.count
-        half = self.count // 2
-        return jnp.where(spot < half, 2 * spot, 2 * (self.count - 1 - spot) + 1)
-
-    def gather(self, own):
-        half = self.count // 2
-        blocks = {0: own}
-        ahead = behind = own
-        for step in range(1, half):
-            ahead = lax.ppermute(ahead, "head", self.forward)
-            behind = lax.ppermute(behind, "head", self.backward)
-            blocks[-step], blocks[step] = ahead, behind
-        cut = own.shape[-1] // 2
-        left = lax.ppermute(ahead[..., :cut], "head", self.forward)
-        right = lax.ppermute(behind[..., cut:], "head", self.backward)
-        blocks[half] = jnp.concatenate([left, right], axis=-1)
-        return blocks
-
-    def scatter(self, block):
-        half = self.count // 2
-        far = block(half)
-        cut = far.shape[-1] // 2
-        ahead = lax.ppermute(far[..., :cut], "head", self.forward)
-        behind = lax.ppermute(far[..., cut:], "head", self.backward)
-        for step in range(half - 1, 0, -1):
-            give_ahead, give_behind = block(step), block(-step)
-            if step == half - 1:
-                give_ahead = jnp.concatenate(
-                    [add(give_ahead[..., :cut], ahead), give_ahead[..., cut:]], axis=-1
-                )
-                give_behind = jnp.concatenate(
-                    [give_behind[..., :cut], add(give_behind[..., cut:], behind)], axis=-1
+        return jnp.where(spot < self.half, 2 * spot, 2 * (self.count - 1 - spot) + 1)
+
+    def send(self, name, ahead, behind):
+        with jax.named_scope(name):
+            return (
+                lax.ppermute(ahead, "head", self.forward),
+                lax.ppermute(behind, "head", self.backward),
+            )
+
+
+class Gather:
+    def __init__(self, name, ring, own):
+        self.name, self.ring, self.blocks, self.taken = name, ring, {0: own}, 0
+        self.edge = (own, own)
+
+    def settle(self, *gates):
+        *self.edge, _ = lax.optimization_barrier((*self.edge, gates))
+        if 0 < self.taken < self.ring.half:
+            self.blocks[-self.taken], self.blocks[self.taken] = self.edge
+        elif self.taken:
+            self.blocks[self.taken] = tuple(self.edge)
+
+    def step(self, *gates):
+        self.settle(*gates)
+        self.taken += 1
+        ahead, behind = self.given = tuple(self.edge)
+        if self.taken == self.ring.half:
+            cut = ahead.shape[-1] // 2
+            self.edge = self.ring.send(self.name, ahead[..., :cut], behind[..., cut:])
+            self.blocks[self.taken] = self.edge
+        else:
+            self.edge = self.ring.send(self.name, ahead, behind)
+            self.blocks[-self.taken], self.blocks[self.taken] = self.edge
+        return self.edge
+
+    def last_steps(self, *gates):
+        while self.taken < self.ring.half:
+            self.step(*gates)
+            gates = ()
+        return self.blocks
+
+
+class Scatter:
+    def __init__(self, name, ring, block):
+        self.name, self.ring, self.block, self.taken = name, ring, block, 0
+
+    def step(self, *gates):
+        left = self.ring.half - self.taken
+        if self.taken == 0:
+            far = after(self.block(left), *gates)
+            cut = far.shape[-1] // 2
+            give = far[..., :cut], far[..., cut:]
+        else:
+            give = self.block(left), self.block(-left)
+            ahead, behind, _ = lax.optimization_barrier((*self.edge, gates))
+            cut = ahead.shape[-1]
+            if self.taken == 1:
+                give = (
+                    jnp.concatenate([add(give[0][..., :cut], ahead), give[0][..., cut:]], axis=-1),
+                    jnp.concatenate([give[1][..., :cut], add(give[1][..., cut:], behind)], axis=-1),
                 )
             else:
-                give_ahead, give_behind = add(give_ahead, ahead), add(give_behind, behind)
-            ahead = lax.ppermute(give_ahead, "head", self.forward)
-            behind = lax.ppermute(give_behind, "head", self.backward)
-        return wide(block(0)) + wide(ahead) + wide(behind)
+                give = add(give[0], ahead), add(give[1], behind)
+        self.taken, self.given = self.taken + 1, give
+        self.edge = self.ring.send(self.name, *give)
+        return self.edge
+
+    def settle(self, *gates):
+        *self.edge, _ = lax.optimization_barrier((*self.edge, gates))
+
+    def last_steps(self, *gates):
+        while self.taken < self.ring.half:
+            self.step(*gates)
+            gates = ()
+        return wide(self.block(0)) + wide(self.edge[0]) + wide(self.edge[1])
+
+
+def whole_block(piece):
+    return jnp.concatenate(piece, axis=-1) if isinstance(piece, tuple) else piece
+
+
+def copy_kernel(plan, sources, starts_ref, *refs):
+    inputs, outputs, sems = refs[:sources], refs[sources:-1], refs[-1]
+    copies = []
+    for i, (source, rows, cols, target, slot, target_cols) in enumerate(plan):
+        count = rows[1] - rows[0]
+        start = pl.multiple_of(starts_ref[slot], count)
+        copies.append(
+            pltpu.make_async_copy(
+                inputs[source].at[rows[0] : rows[1], cols[0] : cols[1]],
+                outputs[target].at[pl.ds(start, count), target_cols[0] : target_cols[1]],
+                sems.at[i],
+            )
+        )
+    for copy in copies:
+        copy.start()
+    for copy in copies:
+        copy.wait()
+
+
+def place_blocks(plan, arrays, starts, shapes):
+    anywhere = pl.BlockSpec(memory_space=pl.ANY)
+    moved = 2 * sum(a.size for a in arrays)
+    return pl.pallas_call(
+        functools.partial(copy_kernel, plan, len(arrays)),
+        in_specs=[pl.BlockSpec(memory_space=pltpu.SMEM)]
+        + [pl.BlockSpec(memory_space=pltpu.VMEM)] * len(arrays),
+        out_specs=[anywhere] * len(shapes),
+        out_shape=[jax.ShapeDtypeStruct(s, arrays[0].dtype) for s in shapes],
+        scratch_shapes=[pltpu.SemaphoreType.DMA((len(plan),))],
+        compiler_params=pltpu.CompilerParams(vmem_limit_bytes=40 * 2**20),
+        cost_estimate=pl.CostEstimate(flops=0, bytes_accessed=2 * moved, transcendentals=0),
+        name="place_blocks",
+    )(jnp.stack(starts).astype(jnp.int32), *arrays)
 
 
 def wide(block):
@@ -79,30 +165,51 @@
     return lax.ppermute(block, "dp", [(i, i ^ bit) for i in range(count)])
 
 
-def dp_gather(own):
-    bits = lax.axis_size("dp").bit_length() - 1
-    for bit in reversed(range(bits)):
-        own = jnp.concatenate([own, flip(own, 1 << bit)], axis=0)
+def dp_bits():
+    return lax.axis_size("dp").bit_length() - 1
+
+
+def dp_gather(own, *gates):
+    for bit, gate in zip(reversed(range(dp_bits())), (*gates, *[()] * dp_bits())):
+        got = flip(own, 1 << bit)
+        own, got, _ = lax.optimization_barrier((own, got, gate))
+        own = jnp.concatenate([own, got], axis=0)
     return own
 
 
 def dp_bit_order():
-    bits = lax.axis_size("dp").bit_length() - 1
     order = [0]
-    for bit in reversed(range(bits)):
+    for bit in reversed(range(dp_bits())):
         order = order + [r | 1 << bit for r in order]
     return order
 
 
-def dp_scatter(blocks):
-    bits = lax.axis_size("dp").bit_length() - 1
-    for bit in range(bits):
+def dp_scatter_step(blocks, distance, *gates):
+    half = blocks.shape[0] // 2
+    return add(blocks[:half], after(flip(blocks[half:], distance), *gates))
+
+
+def dp_scatter(blocks, distance=1, *gates):
+    while distance < lax.axis_size("dp"):
+        blocks = dp_scatter_step(blocks, distance, *gates)
+        distance *= 2
+    return blocks
+
+
+def dp_scatter_cols(blocks):
+    for bit in range(dp_bits()):
+        half = blocks.shape[1] // 2
+        blocks = add(blocks[:, :half], flip(blocks[:, half:], 1 << bit))
+    return blocks
+
+
+def dp_sum_blocks(blocks):
+    distance = 1
+    while distance < lax.axis_size("dp"):
         half = blocks.shape[0] // 2
-        got = flip(blocks[half:], 1 << bit)
-        if bit == bits - 1:
-            return wide(blocks[:half]) + wide(got)
-        blocks = add(blocks[:half], got)
-    return wide(blocks)
+        blocks = blocks[:half] + flip(blocks[half:], distance)
+        distance *= 2
+    return blocks
 
 
 def dot_last(a, b):
@@ -293,6 +400,7 @@
     share = w_gate.shape[1] // members
     part = width // members
     order = dp_bit_order()
+    offsets = ring.offsets
 
     def own_rows(whole, of=None):
         of = rank if of is None else of
@@ -301,69 +409,118 @@
         return jnp.concatenate([first, second], axis=0)
 
     def place_rows(blocks):
-        whole = jnp.zeros((length, blocks[0].shape[1]), blocks[0].dtype)
+        plan, arrays, starts = [], [], []
         for offset, piece in blocks.items():
             of = ring.owner(offset)
-            whole = lax.dynamic_update_slice_in_dim(whole, piece[:block], of * block, 0)
-            whole = lax.dynamic_update_slice_in_dim(
-                whole, piece[block:], (2 * ranks - 1 - of) * block, 0
-            )
-        return whole
-
+            first = 0
+            for array in piece if isinstance(piece, tuple) else (piece,):
+                last = first + array.shape[1]
+                for slot in range(2):
+                    plan.append(
+                        (
+                            len(arrays),
+                            (slot * block, (slot + 1) * block),
+                            (0, array.shape[1]),
+                            0,
+                            len(starts) + slot,
+                            (first, last),
+                        )
+                    )
+                arrays.append(array)
+                first = last
+            starts += [of * block, (2 * ranks - 1 - of) * block]
+        return place_blocks(plan, arrays, starts, [(length, width)])[0]
+
+    def member_cols(whole):
+        return jnp.concatenate(
+            [lax.dynamic_slice_in_dim(whole, (member ^ r) * part, part, 1) for r in order], axis=1
+        )
+
+    core = member % 2
     packed = jnp.concatenate([w_query.T, w_key.T, w_value.T, w_out], axis=1)
     half_cols = cols // 2
-    core = member % 2
-    blocks = ring.gather(lax.dynamic_slice_in_dim(packed, core * half_cols, half_cols, 0))
-    mine = jnp.zeros((ranks, half_cols, packed.shape[1]), packed.dtype)
-    for offset, piece in blocks.items():
-        mine = lax.dynamic_update_slice_in_dim(mine, piece[None], ring.owner(offset), 0)
-    theirs = flip(mine, 1)
-    first, second = jnp.where(core == 0, mine, theirs), jnp.where(core == 0, theirs, mine)
-    packed = jnp.stack([first, second], axis=1).reshape(ranks * cols, packed.shape[1])
-    query_t = packed[:, :width]
-    key_t = packed[:, width : width + inner]
-    value_t = packed[:, width + inner : width + 2 * inner]
-    out_all = packed[:, width + 2 * inner :]
-
-    gate_own = lax.dynamic_slice_in_dim(w_gate, member * share, share, 1).T
-    up_own = lax.dynamic_slice_in_dim(w_up, member * share, share, 1).T
-    down_own = lax.dynamic_slice_in_dim(w_down, member * share, share, 0)
-    blocks = ring.gather(jnp.concatenate([gate_own, up_own, down_own], axis=0))
-    offsets = list(blocks)
-    gate_t = jnp.concatenate([blocks[o][:share] for o in offsets], axis=0)
-    up_t = jnp.concatenate([blocks[o][share : 2 * share] for o in offsets], axis=0)
-    down = jnp.concatenate([blocks[o][2 * share :] for o in offsets], axis=0)
-
-    labels = jnp.arange(group_weights.shape[0], dtype=jnp.int32)
-    row_weight = jnp.sum(jnp.where(group_ids[0] == labels, group_weights, 0.0))
-    grad_out = wide(own_rows(cotangent)) * row_weight
-    grad_low_all = dp_gather(low(grad_out))
-
+    attn_ring = Gather("attn_weights", ring, lax.dynamic_slice_in_dim(packed, core * half_cols, half_cols, 0))
+    a1 = attn_ring.step()
     inputs = wide(tokens)
     root = lax.rsqrt(jnp.mean(inputs * inputs, axis=-1, keepdims=True) + epsilon)
     normed = low(inputs * root * gain_attn)
-    latent = low(dot_plain(normed, w_latent))
-    half_heads = query_t.shape[0] // 2
-    latents = (latent[:, :inner], latent[:, inner:])
-
-    def from_latents(weight_t):
-        return jnp.concatenate(
-            [
-                low(dot_last(latents[0], weight_t[:half_heads])),
-                low(dot_last(latents[1], weight_t[half_heads:])),
-            ],
-            axis=1,
-        )
-
-    keys, values = from_latents(key_t), from_latents(value_t)
-    inputs_own, root_own, normed_own = own_rows(inputs), own_rows(root), own_rows(normed)
-    queries = low(dot_last(normed_own, query_t))
+    a2 = attn_ring.step(normed)
+    latent = low(dot_plain(after(normed, *a1), w_latent))
+
+    labels = jnp.arange(group_weights.shape[0], dtype=jnp.int32)
+    row_weight = jnp.sum(jnp.where(group_ids[0] == labels, group_weights, 0.0))
+    grad_out = wide(own_rows(after(cotangent, *a1))) * row_weight
+    grad_low = low(grad_out)
+    a3 = attn_ring.step(latent)
+
+    gate_w, up_w, down_w, *_ = lax.optimization_barrier((w_gate, w_up, w_down, *a2))
+    units = jnp.concatenate(
+        [
+            lax.dynamic_slice_in_dim(gate_w, member * share, share, 1).T,
+            lax.dynamic_slice_in_dim(up_w, member * share, share, 1).T,
+            lax.dynamic_slice_in_dim(down_w, member * share, share, 0),
+        ],
+        axis=1,
+    )
+    attn_ring.step(units, grad_low)
+    unit_ring = Gather("mlp_weights", ring, units)
+    w1 = unit_ring.step(*a3)
+
+    blocks = attn_ring.last_steps()
+    mine = jnp.stack([whole_block(blocks[o]) for o in offsets]).reshape(-1, packed.shape[1])
+    theirs = flip(mine, 1)
+    edges = (0, width, width + inner, width + 2 * inner, 2 * width + 2 * inner)
+    plan, starts = [], []
+    for spot, offset in enumerate(offsets):
+        for source in range(2):
+            for target in range(4):
+                plan.append(
+                    (
+                        source,
+                        (spot * half_cols, (spot + 1) * half_cols),
+                        (edges[target], edges[target + 1]),
+                        target,
+                        len(starts),
+                        (0, edges[target + 1] - edges[target]),
+                    )
+                )
+            starts.append(ring.owner(offset) * cols + (core ^ source) * half_cols)
+    query_t, key_t, value_t, out_all = place_blocks(
+        plan,
+        [mine, theirs],
+        starts,
+        [(ranks * cols, edges[t + 1] - edges[t]) for t in range(4)],
+    )
+
+    inputs_own = wide(own_rows(after(tokens, *a2)))
+    root_own = lax.rsqrt(jnp.mean(inputs_own * inputs_own, axis=-1, keepdims=True) + epsilon)
+    normed_own = low(inputs_own * root_own * gain_attn)
     rank_ref = rank.astype(jnp.int32).reshape(1)
-    mixed, lse = attention_forward(rank_ref, ranks, queries, keys, values)
-    hidden = inputs_own + dot_plain(mixed, out_all)
+    groups = [
+        (slice(j * width // 2, (j + 1) * width // 2), latent[:, j * inner : (j + 1) * inner])
+        for j in range(2)
+    ]
+    kept, mixed = [], ()
+    for s, latent_j in groups:
+        latent_j, normed_j, _ = lax.optimization_barrier((latent_j, normed_own, mixed))
+        keys = low(dot_last(latent_j, key_t[s]))
+        values = low(dot_last(latent_j, value_t[s]))
+        queries = low(dot_last(normed_j, query_t[s]))
+        if not kept:
+            queries = after(queries, *w1)
+            w2 = unit_ring.step()
+        mixed, lse = attention_forward(rank_ref, ranks, queries, keys, values)
+        kept.append((queries, keys, values, mixed, lse))
+    w3 = unit_ring.step(mixed)
+    grad_low_all = dp_gather(grad_low, kept[0][3], kept[1][3])
+    hidden = inputs_own + dot_plain(kept[0][3], out_all[groups[0][0]])
+    hidden += dot_plain(kept[1][3], out_all[groups[1][0]])
 
     root_mlp = lax.rsqrt(jnp.mean(hidden * hidden, axis=-1, keepdims=True) + epsilon)
-    normed_mlp = dp_gather(low(hidden * root_mlp * gain_mlp))
+    normed_mlp = dp_gather(low(hidden * root_mlp * gain_mlp), w3)
+    blocks = unit_ring.last_steps()
+    units = jnp.concatenate([whole_block(blocks[o]) for o in offsets], axis=0)
+    gate_t, up_t, down = units[:, :width], units[:, width : 2 * width], units[:, 2 * width :]
     gate = dot_last(normed_mlp, gate_t)
     up = dot_last(normed_mlp, up_t)
     logistic = jax.nn.sigmoid(gate)
@@ -371,21 +528,25 @@
     grad_act = dot_last(grad_low_all, down)
     grad_gate = low(grad_act * up * logistic * (1.0 + gate * (1.0 - logistic)))
     grad_up = low(grad_act * gate * logistic)
-    grad_normed_mlp = dp_scatter(low(dot_plain(grad_gate, gate_t) + dot_plain(grad_up, up_t)))
-    mlp_out = dp_scatter(low(dot_plain(act, down)))
-    block_out = place_rows(ring.gather(low(hidden + mlp_out)))
-
-    grad_w_gate = low(contract_rows(grad_gate, normed_mlp))
-    grad_w_up = low(contract_rows(grad_up, normed_mlp))
-    grad_w_down = low(contract_rows(act, grad_low_all))
-
-    def mlp_block(offset):
+    normed_part = low(dot_plain(grad_gate, gate_t) + dot_plain(grad_up, up_t))
+    normed_sum = dp_scatter_step(normed_part, 1)
+    mlp_sum = dp_scatter_step(after(low(dot_plain(act, down)), normed_sum), 1)
+    grad_gate, grad_up, act, *_ = lax.optimization_barrier((grad_gate, grad_up, act, mlp_sum))
+    grad_units = jnp.concatenate(
+        [
+            low(contract_rows(grad_gate, normed_mlp)),
+            low(contract_rows(grad_up, normed_mlp)),
+            low(contract_rows(act, grad_low_all)),
+        ],
+        axis=1,
+    )
+
+    def unit_rows(offset):
         spot = offsets.index(offset)
-        rows = slice(spot * share, (spot + 1) * share)
-        return jnp.concatenate([grad_w_gate[rows], grad_w_up[rows], grad_w_down[rows]], axis=0)
-
-    mlp_grads = low(ring.scatter(mlp_block)).reshape(3, share, width)
-    mlp_grads = wide(lax.all_to_all(mlp_grads, "dp", 2, 1, tiled=True))
+        return grad_units[spot * share : (spot + 1) * share]
+
+    unit_sums = Scatter("mlp_grads", ring, unit_rows)
+    r1 = unit_sums.step()
 
     def norm_backward(incoming, gain, entered, scale):
         scaled = gain * incoming
@@ -393,63 +554,73 @@
         grad = scale * scaled - entered * (scale * scale * scale) * inner_mean
         return grad, jnp.sum(incoming * entered * scale, axis=0)
 
-    grad_hidden, grad_gain_mlp = norm_backward(grad_normed_mlp, gain_mlp, hidden, root_mlp)
+    incoming = wide(dp_scatter(normed_sum, 2, grad_units))
+    grad_hidden, grad_gain_mlp = norm_backward(incoming, gain_mlp, hidden, root_mlp)
     grad_hidden = grad_out + grad_hidden
     grad_hidden_low = low(grad_hidden)
-    grad_mixed = low(dot_last(grad_hidden_low, out_all))
-
-    def member_cols(whole, r):
-        return lax.dynamic_slice_in_dim(whole, (member ^ order[r]) * part, part, 1)
-
-    def by_member(left, right):
-        return jnp.concatenate(
-            [low(contract_rows(left, member_cols(right, r))) for r in range(members)], axis=0
+    r2 = unit_sums.step(grad_hidden_low)
+    mlp_out = dp_scatter(after(mlp_sum, grad_hidden_low), 2)
+
+    grads = []
+    grad_hidden_late = after(grad_hidden_low, *r1)
+    before = ()
+    for (s, latent_j), (queries, keys, values, mixed, lse) in zip(groups, kept):
+        grad_mixed = after(low(dot_last(grad_hidden_late, out_all[s])), *before)
+        grads.append(
+            attention_backward(rank_ref, ranks, queries, keys, values, mixed, grad_mixed, lse)
         )
-
-    grad_w_out = low(dp_scatter(by_member(mixed, grad_hidden_low)))
-
-    grad_queries, grad_keys, grad_values = attention_backward(
-        rank_ref, ranks, queries, keys, values, mixed, grad_mixed, lse
-    )
-    grad_latent = jnp.concatenate(
-        [
-            low(
-                dot_plain(grad_keys[:, s], key_t[s]) + dot_plain(grad_values[:, s], value_t[s])
-            )
-            for s in (slice(0, half_heads), slice(half_heads, None))
-        ],
-        axis=1,
-    )
-    grad_latent_own = low(ring.scatter(lambda o: own_rows(grad_latent, ring.owner(o))))
-    grad_normed = dot_plain(grad_queries, query_t) + dot_last(grad_latent_own, w_latent)
+        if len(grads) == 1:
+            before = (*r2, grads[0][0])
+            r3 = unit_sums.step(grads[0][0], mlp_out)
+    r4 = unit_sums.step(r2, grads[1][0])
+    grads, _ = lax.optimization_barrier((grads, unit_sums.given))
+    grad_latent = [
+        low(dot_plain(g[1], key_t[s]) + dot_plain(g[2], value_t[s]))
+        for (s, _), g in zip(groups, grads)
+    ]
+    grad_latent = jnp.concatenate(grad_latent, axis=1)
+    latent_sums = Scatter("latent_grads", ring, lambda o: own_rows(grad_latent, ring.owner(o)))
+    block_ring = Gather("block_out", ring, low(hidden + mlp_out))
+    edge = (*r4, *latent_sums.step())
+    hidden_late = after(grad_hidden_low, latent_sums.given)
+    for _ in range(ring.half - 1):
+        edge = (*latent_sums.step(*edge), *block_ring.step(*edge))
+    block_ring.last_steps(*edge)
+    grad_latent_own = low(latent_sums.last_steps())
+    grad_normed = dot_last(grad_latent_own, w_latent)
+    for (s, _), g in zip(groups, grads):
+        grad_normed += dot_plain(g[0], query_t[s])
     grad_inputs, grad_gain_attn = norm_backward(grad_normed, gain_attn, inputs_own, root_own)
-    grad_tokens = place_rows(ring.gather(low(grad_hidden + grad_inputs)))
-
-    grad_w_query = by_member(grad_queries, normed_own)
-    grad_w_latent = by_member(grad_latent_own, normed_own)
-    rows_query = query_t.shape[0]
-    rows_latent = w_latent.shape[1]
-    joint = dp_scatter(
+    gain_rows = jnp.stack([low(grad_gain_attn), low(grad_gain_mlp)])
+    gain_rows = jnp.concatenate([gain_rows, jnp.zeros((14, width), jnp.bfloat16)], axis=0)
+    token_ring = Gather(
+        "grad_tokens",
+        ring,
+        jnp.concatenate([low(grad_hidden + grad_inputs), gain_rows], axis=0),
+    )
+    edge = (*token_ring.step(), *block_ring.edge)
+    unit_sums.settle(token_ring.given)
+    mlp_grads = low(unit_sums.last_steps()).reshape(share, 3, width)
+    mlp_grads = wide(lax.all_to_all(mlp_grads, "dp", 2, 0, tiled=True))
+    block_out = place_rows(block_ring.blocks)
+
+    hidden_cols = member_cols(hidden_late)
+    normed_cols = member_cols(normed_own)
+    grad_w_out = dp_scatter_cols(
+        jnp.concatenate([low(contract_rows(k[3], hidden_cols)) for k in kept], axis=0)
+    )
+    lefts = (grads[0][0], grads[1][0], grad_latent_own)
+    joint = dp_scatter_cols(
+        jnp.concatenate([low(contract_rows(left, normed_cols)) for left in lefts], axis=0)
+    )
+    inner_part = inner // members
+    grad_w_kv = [
         jnp.concatenate(
-            [
-                grad_w_query.reshape(members, rows_query, part),
-                grad_w_latent.reshape(members, rows_latent, part),
-            ],
+            [low(contract_rows(latent_j, g[i])) for (_, latent_j), g in zip(groups, grads)],
             axis=1,
         )
-    )
-    joint = low(joint[0])
-    grad_w_kv = [
-        jnp.concatenate(
-            [
-                low(contract_rows(latents[0], grad[:, :half_heads])),
-                low(contract_rows(latents[1], grad[:, half_heads:])),
-            ],
-            axis=1,
-        )
-        for grad in (grad_keys, grad_values)
+        for i in (1, 2)
     ]
-    inner_part = inner // members
     kv = low(
         dp_scatter(
             jnp.concatenate(
@@ -462,26 +633,45 @@
             )
         )
     )
-    latent_cols = rows_latent // ranks
+    grad_w_out, joint = low(grad_w_out), low(joint)
+    latent_cols = w_latent.shape[1] // ranks
+    side_by_side = 2 * cols == part
 
     def attn_block(offset):
         of = ring.owner(offset)
-        kv_piece = lax.dynamic_slice_in_dim(kv, of * cols, cols, 1).reshape(-1, part)
+        kv_piece = lax.dynamic_slice_in_dim(kv, of * cols, cols, 1)
+        if side_by_side:
+            kv_piece = jnp.concatenate([kv_piece[:inner_part], kv_piece[inner_part:]], axis=1)
         return jnp.concatenate(
             [
                 lax.dynamic_slice_in_dim(grad_w_out, of * cols, cols, 0),
                 lax.dynamic_slice_in_dim(joint, of * cols, cols, 0),
-                lax.dynamic_slice_in_dim(joint, rows_query + of * latent_cols, latent_cols, 0),
-                kv_piece,
+                lax.dynamic_slice_in_dim(joint, ranks * cols + of * latent_cols, latent_cols, 0),
+                kv_piece.reshape(-1, part),
             ],
             axis=0,
         )
 
-    attn_grads = ring.scatter(attn_block)
-    kv_grads = attn_grads[2 * cols + latent_cols :].reshape(2, inner_part, cols)
-
-    gains = lax.psum(jnp.stack([grad_gain_attn, grad_gain_mlp]), ("head", "dp"))
-    gains = lax.dynamic_slice_in_dim(gains, member * part, part, 1)
+    attn_sums = Scatter("attn_grads", ring, attn_block)
+    for step in range(ring.half - 1):
+        edge = (*token_ring.step(*edge), *attn_sums.step(*edge))
+        if step == 0:
+            edge = (*edge, block_out)
+    attn_grads = attn_sums.last_steps(*edge)
+    kv_grads = attn_grads[2 * cols + latent_cols :]
+    if side_by_side:
+        kv_grads = kv_grads[:, :cols], kv_grads[:, cols:]
+    else:
+        kv_grads = kv_grads.reshape(2, inner_part, cols)
+    grad_tokens = place_rows(token_ring.last_steps())
+
+    gains = sum(
+        wide(whole_block(piece)[2 * block : 2 * block + 2]) for piece in token_ring.blocks.values()
+    )
+    gains = jnp.stack(
+        [lax.dynamic_slice_in_dim(gains, (member ^ r) * part, part, 1) for r in order]
+    )
+    gains = dp_sum_blocks(gains)[0]
     return (
         block_out,
         grad_tokens,
@@ -492,9 +682,9 @@
         kv_grads[1],
         attn_grads[:cols],
         gains[1],
-        mlp_grads[0].T,
-        mlp_grads[1].T,
-        mlp_grads[2],
+        mlp_grads[:, 0].T,
+        mlp_grads[:, 1].T,
+        mlp_grads[:, 2],
     )
 
 

time: 466 us -> 369 us (0.79)
  blocking collectives: 43.4 us -> 0 us
  local copies, waits for them, and re-layouts: 86.1 us -> 53 us
  other arithmetic: 54.1 us -> 35.5 us
  Pallas kernels: 41.4 us -> 52.9 us
  waiting for transfers between devices: 113 us -> 105 us
  matrix products: 44.7 us -> 38 us
    psum x1 -> x0, blocking collectives: 43.4 us -> none  [body(): gains = lax.psum(jnp.stack([grad_gain_attn, grad_gain_mlp]), ('head', 'dp'))]
    dynamic_update_slice x38 -> x0, local copies, waits for them, and re-layouts: 37.5 us -> none  [the longest x16 16.5 us: place_rows(): whole = lax.dynamic_update_slice_in_dim(whole, piece[:block], of * block, 0)]
    concatenate x22 -> x15, other arithmetic: 15.6 us -> 4.23 us  [the longest x3 1.61 us: step(): jnp.concatenate([give[1][..., :cut], add(give[1][..., cut:], behind)], ax...]
    pallas_call x0 -> x3, Pallas kernels: none -> 10.9 us  [place_blocks(): pl.pallas_call(functools.partial(copy_kernel, plan, len(arrays)), in_spec...]
    slice x29 -> x23, local copies, waits for them, and re-layouts: 14 us -> 6.38 us  [the longest x5 2.04 us: dp_scatter_step(): return add(blocks[:half], after(flip(blocks[half:], distance), *gates))]
    ppermute x15 -> x17, waiting for transfers between devices: 22.5 us -> 15 us  [flip(): return lax.ppermute(block, 'dp', [(i, i ^ bit) for i in range(count)])]
    dot_general x19 -> x12, matrix products: 15.5 us -> 10.2 us  [contract_rows(): lax.dot_general(left, right, (((0,), (0,)), ((), ())), preferred_element_...]
    convert_element_type x23, other arithmetic: 16 us -> 11.1 us  [add(): return (wide(left) + wide(right)).astype(jnp.bfloat16)]
  transfers between devices with their start and end apart: 72 -> 74, of which waited for: 32 -> 35; matrix products, arithmetic and copies ran while one was open for 32% -> 26% of each run, Pallas kernels for 9% -> 15%
where the time goes in v2:
time: 369 us; the launch traced here: 362 us
  waiting for transfers between devices  105 us (28%)
  starting transfers between devices  73.6 us (20%)
  local copies, waits for them, and re-layouts  53 us (14%)
  Pallas kernels  52.9 us (14%)
  matrix products  38 us (10%)
  other arithmetic  35.5 us (10%)
  between operations  4.02 us (1%)
    ppermute x28, waiting for transfers between devices, send(): lax.ppermute(ahead, 'head', self.forward)  49.1 us
    ppermute x28, waiting for transfers between devices, send(): lax.ppermute(behind, 'head', self.backward)  41.4 us
    ppermute x28, starting transfers between devices, send(): lax.ppermute(behind, 'head', self.backward)  30.2 us
    ppermute x28, starting transfers between devices, send(): lax.ppermute(ahead, 'head', self.forward)  29.5 us
    pallas_call x2, Pallas kernels, attention_backward(): pl.pallas_call(functools.partial(bwd_kernel, ranks, step), grid=(pairs,),...  25.9 us
    unnamed x230, local copies, waits for them, and re-layouts  21.7 us
    pallas_call x2, Pallas kernels, attention_forward(): pl.pallas_call(functools.partial(fwd_kernel, ranks), grid=(pairs,), in_sp...  16 us
    dot_general x12, matrix products, dot_plain(): return jnp.dot(a, b, preferred_element_type=jnp.float32)  15 us
  transfers between devices with their start and end apart: 74, of which 35 were waited for; matrix products, arithmetic and copies ran while one was open for 26% of the time, Pallas kernels for 15%

profile of v2, /device:TPU:0, one launch (start us, length us, event | category | flops | bytes accessed | tf_op | source)
XLA Modules:
  0.0 362.5 jit_solution(8289670748262888396)
XLA Ops:
  3.8 1.7 bitcast_dynamic-update-slice_fusion.6
  5.4 3.0 collective-permute-start
  8.5 3.1 fusion
  11.6 2.6 fusion.2
  16.1 1.7 collective-permute-done.1
  20.5 1.7 bitcast_dynamic-update-slice_fusion.4
  22.2 4.5 %convolution_convert_fusion.4 = bf16[2048,512]{1,0:T(8,128)(2,1)S(1)} fusion(bf16[2048,1024]{1,0:T(8,128)(2,1)} %fusion.2, bf16[1024,512]{1,0:T(8,128)(2,1)S(1)} %copy-done), kind=kOutput, calls=%fused_computation.45 | convolution fusion | flops 2148532224 | bytes 7340032 | tf_op jit(solution)/shard_map/dot_general | solution.py:219
  43.1 2.5 collective-permute-done.6
  54.0 10.4 %collective-permute-done.10 = bf16[88,3072]{1,0:T(8,128)(2,1)} collective-permute-done((bf16[88,3072]{1,0:T(8,128)(2,1)S(1)}, bf16[88,3072]{1,0:T(8,128)(2,1)}, u32[]{:S(2)}, u32[]{:S(2)}) %collective-permute-start.10) | collective-permute-done | bytes 540704 | tf_op jit(solution)/shard_map/mlp_weights/ppermute | solution.py:45
  66.8 1.9 constant_dynamic-update-slice_fusion.9
  68.7 1.9 constant_dynamic-update-slice_fusion.8
  70.5 4.1 %place_blocks.3 = (bf16[1024,1024]{1,0:T(8,128)(2,1)S(1)}, bf16[1024,256]{1,0:T(8,128)(2,1)S(1)}, bf16[1024,256]{1,0:T(8,128)(2,1)S(1)}, bf16[1024,1024]{1,0:T(8,128)(2,1)S(1)}) custom-call(s32[16]{0:T(128)S(1)} %stack.201.starts_ref, bf16[512,2560]{1,0:T(8,128)(2,1)} %bitcast.47.refs_0_, bf16[512,2560]{1,0:T(8,128)(2,1)} %collective-permute-done.8.refs_1_), custom_call_target="tpu_custom_call" | custom-call | bytes 10485760 | tf_op jit(solution)/shard_map/place_blocks/pallas_call | solution.py:142
  77.2 8.0 %attention_forward.2 = (bf16[256,512]{1,0:T(8,128)(2,1)S(1)}, f32[4,8,256]{2,1,0:T(8,128)S(1)}) custom-call(s32[1]{0:T(128)} %bitcast.19.rank_ref, bf16[256,512]{1,0:T(8,128)(2,1)S(1)} %convolution_convert_fusion.21.q_ref, bf16[2048,512]{1,0:T(8,128)(2,1)S(1)} %convolution_convert_fusion.3.k_ref, bf16[2048,512]{1,0:T(8,128)(2,1)S(1)} %convolution_convert_fusion.2.v_ref), custom_call_target="tpu_custom_call" | custom-call | flops 1073741824 | bytes 4194304 | tf_op jit(solution)/shard_map/attention_forward/pallas_call | solution.py:281
  87.4 8.0 %attention_forward.3 = (bf16[256,512]{1,0:T(8,128)(2,1)S(1)}, f32[4,8,256]{2,1,0:T(8,128)S(1)}) custom-call(s32[1]{0:T(128)} %bitcast.19.rank_ref, bf16[256,512]{1,0:T(8,128)(2,1)S(1)} %convolution_convert_fusion.20.q_ref, bf16[2048,512]{1,0:T(8,128)(2,1)S(1)} %convolution_convert_fusion.1.k_ref, bf16[2048,512]{1,0:T(8,128)(2,1)S(1)} %convolution_convert_fusion.v_ref), custom_call_target="tpu_custom_call" | custom-call | flops 1073741824 | bytes 4194304 | tf_op jit(solution)/shard_map/attention_forward/pallas_call | solution.py:281
  101.6 8.1 %collective-permute-done.11 = bf16[256,1024]{1,0:T(8,128)(2,1)S(1)} collective-permute-done((bf16[256,1024]{1,0:T(8,128)(2,1)S(1)}, bf16[256,1024]{1,0:T(8,128)(2,1)S(1)}, u32[]{:S(2)}, u32[]{:S(2)}) %collective-permute-start.11) | collective-permute-done | bytes 524320 | tf_op jit(solution)/shard_map/ppermute | solution.py:165
  114.8 6.7 %collective-permute-done.17 = bf16[88,1536]{1,0:T(8,128)(2,1)S(1)} collective-permute-done((bf16[88,1536]{1,0:T(8,128)(2,1)S(1)}, bf16[88,1536]{1,0:T(8,128)(2,1)S(1)}, u32[]{:S(2)}, u32[]{:S(2)}) %collective-permute-start.17) | collective-permute-done | bytes 270368 | tf_op jit(solution)/shard_map/mlp_weights/ppermute | solution.py:44
  122.9 1.7 fusion.7
  124.8 1.7 fusion.12
  126.5 3.7 %multiply_convert_fusion.1 = (bf16[1024,704]{0,1:T(8,128)(2,1)S(1)}, bf16[1024,704]{0,1:T(8,128)(2,1)S(1)}, bf16[1024,704]{0,1:T(8,128)(2,1)S(1)}) fusion(f32[1024,704]{0,1:T(8,128)S(1)} %fusion.7, f32[1024,704]{0,1:T(8,128)S(1)} %fusion.12, bf16[1024,1024]{1,0:T(8,128)(2,1)S(1)} %constant_dynamic-update-slice_fusion.2, ...), kind=kOutput, calls=%fused_computation.47 | convolution fusion | flops 1487929344 | bytes 13631488 | tf_op jit(solution)/shard_map/dot_general | solution.py:216
  130.2 1.8 fusion.10
  132.1 2.0 add_convert_fusion
  134.2 1.8 convolution_convert_fusion.5
  141.3 1.9 add_convert_fusion.3
  143.3 1.7 convolution_convert_fusion.8
  145.0 1.7 convolution_convert_fusion.7
  147.0 1.7 convolution_convert_fusion.6
  151.4 2.2 collective-permute-done.23
  153.9 2.0 fusion.109
  161.3 13.0 %attention_backward.2 = (bf16[256,512]{1,0:T(8,128)(2,1)S(1)}, bf16[2048,512]{1,0:T(8,128)(2,1)S(1)}, bf16[2048,512]{1,0:T(8,128)(2,1)S(1)}) custom-call(s32[1]{0:T(128)} %bitcast.19.rank_ref, bf16[256,512]{1,0:T(8,128)(2,1)S(1)} %copy-done.26, bf16[2048,512]{1,0:T(8,128)(2,1)} %copy-done.4, bf16[2048,512]{1,0:T(8,128)(2,1)} %copy-done.3, ...), custom_call_target="tpu_custom_call" | custom-call | flops 2684354560 | bytes 8388608 | tf_op jit(solution)/shard_map/attention_backward/pallas_call | solution.py:348
  180.9 12.9 %attention_backward.3 = (bf16[256,512]{1,0:T(8,128)(2,1)S(1)}, bf16[2048,512]{1,0:T(8,128)(2,1)S(1)}, bf16[2048,512]{1,0:T(8,128)(2,1)S(1)}) custom-call(s32[1]{0:T(128)} %bitcast.19.rank_ref, bf16[256,512]{1,0:T(8,128)(2,1)S(1)} %copy-done.24, bf16[2048,512]{1,0:T(8,128)(2,1)} %copy-done.2, bf16[2048,512]{1,0:T(8,128)(2,1)} %copy-done.1, ...), custom_call_target="tpu_custom_call" | custom-call | flops 2684354560 | bytes 8388608 | tf_op jit(solution)/shard_map/attention_backward/pallas_call | solution.py:348
  215.7 4.8 %collective-permute-done.38 = bf16[256,512]{0,1:T(8,128)(2,1)S(1)} collective-permute-done((bf16[256,512]{0,1:T(8,128)(2,1)S(1)}, bf16[256,512]{0,1:T(8,128)(2,1)S(1)}, u32[]{:S(2)}, u32[]{:S(2)}) %collective-permute-start.38) | collective-permute-done | bytes 262176 | tf_op jit(solution)/shard_map/latent_grads/ppermute | solution.py:45
  220.5 8.9 %collective-permute-done.37 = bf16[256,512]{0,1:T(8,128)(2,1)S(1)} collective-permute-done((bf16[256,512]{0,1:T(8,128)(2,1)S(1)}, bf16[256,512]{0,1:T(8,128)(2,1)S(1)}, u32[]{:S(2)}, u32[]{:S(2)}) %collective-permute-start.37) | collective-permute-done | bytes 262176 | tf_op jit(solution)/shard_map/latent_grads/ppermute | solution.py:44
  234.1 4.7 %collective-permute-done.42 = bf16[256,512]{0,1:T(8,128)(2,1)S(1)} collective-permute-done((bf16[256,512]{0,1:T(8,128)(2,1)S(1)}, bf16[256,512]{0,1:T(8,128)(2,1)S(1)}, u32[]{:S(2)}, u32[]{:S(2)}) %collective-permute-start.42) | collective-permute-done | bytes 262176 | tf_op jit(solution)/shard_map/latent_grads/ppermute | solution.py:45
  240.0 7.0 %collective-permute-done.41 = bf16[256,512]{0,1:T(8,128)(2,1)S(1)} collective-permute-done((bf16[256,512]{0,1:T(8,128)(2,1)S(1)}, bf16[256,512]{0,1:T(8,128)(2,1)S(1)}, u32[]{:S(2)}, u32[]{:S(2)}) %collective-permute-start.41) | collective-permute-done | bytes 262176 | tf_op jit(solution)/shard_map/latent_grads/ppermute | solution.py:44
  251.0 2.5 collective-permute-done.46
  256.6 2.5 collective-permute-done.54
  269.0 5.9 %collective-permute-done.43.refs_5_ = bf16[256,1024]{1,0:T(8,128)(2,1)S(1)} collective-permute-done((bf16[256,1024]{1,0:T(8,128)(2,1)S(1)}, bf16[256,1024]{1,0:T(8,128)(2,1)S(1)}, u32[]{:S(2)}, u32[]{:S(2)}) %collective-permute-start.43) | collective-permute-done | bytes 524320 | tf_op jit(solution)/shard_map/block_out/ppermute | solution.py:44
  279.2 2.1 add_convert_fusion.6
  281.3 2.6 reshape.105
  283.9 3.4 copy.59
  287.3 4.2 %all-to-all-start = ((bf16[88,3,1024]{0,1,2:T(4,128)(2,1)}), bf16[88,3,1024]{0,1,2:T(4,128)(2,1)}, u32[]{:S(2)}, u32[]{:S(2)}) async-start(bf16[88,3,1024]{0,1,2:T(4,128)(2,1)} %copy.59), calls=%async_computation | async-start | bytes 2097152 | tf_op jit(solution)/shard_map/all_to_all | solution.py:604
  295.8 3.2 place_blocks.4
  306.1 8.7 %collective-permute-done.51.refs_3_ = bf16[272,1024]{1,0:T(8,128)(2,1)S(1)} collective-permute-done((bf16[272,1024]{1,0:T(8,128)(2,1)}, bf16[272,1024]{1,0:T(8,128)(2,1)S(1)}, u32[]{:S(2)}, u32[]{:S(2)}) %collective-permute-start.51) | collective-permute-done | bytes 557088 | tf_op jit(solution)/shard_map/grad_tokens/ppermute | solution.py:44
  322.5 2.3 copy.60
  324.8 2.6 reshape.107
  329.0 6.7 %collective-permute-done.64 = bf16[384,256]{1,0:T(8,128)(2,1)} collective-permute-done((bf16[384,256]{1,0:T(8,128)(2,1)}, bf16[384,256]{1,0:T(8,128)(2,1)}, u32[]{:S(2)}, u32[]{:S(2)}) %collective-permute-start.64) | collective-permute-done | bytes 196640 | tf_op jit(solution)/shard_map/attn_grads/ppermute | solution.py:45
  344.7 4.3 %collective-permute-done.69 = bf16[384,256]{1,0:T(8,128)(2,1)S(1)} collective-permute-done((bf16[384,256]{1,0:T(8,128)(2,1)S(1)}, bf16[384,256]{1,0:T(8,128)(2,1)S(1)}, u32[]{:S(2)}, u32[]{:S(2)}) %collective-permute-start.69) | collective-permute-done | bytes 196640 | tf_op jit(solution)/shard_map/attn_grads/ppermute | solution.py:44
  353.8 3.5 place_blocks.5
  (496 shorter events, 158.8 us)
Async XLA Ops:
  5.4 10.6 %collective-permute-start = (bf16[64,2560]{1,0:T(8,128)(2,1)S(1)}, bf16[64,2560]{1,0:T(8,128)(2,1)S(1)}, u32[]{:S(2)}, u32[]{:S(2)}) collective-permute-start(bf16[64,2560]{1,0:T(8,128)(2,1)S(1)} %get-tuple-element.114), channel_id=1, source_target_pairs={{0,8},{8,16},{16,24},{24,28},{28,20},{20,12},{12,4},{4,0},{1,9},{9... | collective-permute-start | bytes 983048 | tf_op jit(solution)/shard_map/attn_weights/ppermute | solution.py:44
  17.7 12.7 %collective-permute-start.2 = (bf16[64,2560]{1,0:T(8,128)(2,1)S(1)}, bf16[64,2560]{1,0:T(8,128)(2,1)S(1)}, u32[]{:S(2)}, u32[]{:S(2)}) collective-permute-start(bf16[64,2560]{1,0:T(8,128)(2,1)S(1)} %collective-permute-done), channel_id=1, source_target_pairs={{0,8},{8,16},{16,24},{24,28},{28,20},{20,12},{12,4},{4,0},{1,9},{9... | collective-permute-start | bytes 983048 | tf_op jit(solution)/shard_map/attn_weights/ppermute | solution.py:44
  19.3 11.1 %collective-permute-start.3 = (bf16[64,2560]{1,0:T(8,128)(2,1)}, bf16[64,2560]{1,0:T(8,128)(2,1)S(1)}, u32[]{:S(2)}, u32[]{:S(2)}) collective-permute-start(bf16[64,2560]{1,0:T(8,128)(2,1)} %collective-permute-done.1), channel_id=1, source_target_pairs={{8,0},{16,8},{24,16},{28,24},{20,28},{12,20},{4,12},{0,4},{9,1},{1... | collective-permute-start | bytes 983048 | tf_op jit(solution)/shard_map/attn_weights/ppermute | solution.py:45
  48.0 22.6 %collective-permute-start.8 = (bf16[512,2560]{1,0:T(8,128)(2,1)}, bf16[512,2560]{1,0:T(8,128)(2,1)}, u32[]{:S(2)}, u32[]{:S(2)}) collective-permute-start(bf16[512,2560]{1,0:T(8,128)(2,1)} %bitcast.47.refs_0_), channel_id=1, source_target_pairs={{0,1},{1,0},{2,3},{3,2},{4,5},{5,4},{6,7},{7,6},{8,9},{9,8},{10,11... | collective-permute-start | bytes 7864328 | tf_op jit(solution)/shard_map/ppermute | solution.py:165
  48.1 52.3 %collective-permute-start.19 = (bf16[256,1024]{1,0:T(8,128)(2,1)}, bf16[256,1024]{1,0:T(8,128)(2,1)}, u32[]{:S(2)}, u32[]{:S(2)}) collective-permute-start(bf16[256,1024]{1,0:T(8,128)(2,1)} %fusion.37), channel_id=1, source_target_pairs={{0,2},{1,3},{2,0},{3,1},{4,6},{5,7},{6,4},{7,5},{8,10},{9,11},{10,... | collective-permute-start | bytes 1572872 | tf_op jit(solution)/shard_map/ppermute | solution.py:165
  49.8 14.6 %collective-permute-start.10 = (bf16[88,3072]{1,0:T(8,128)(2,1)S(1)}, bf16[88,3072]{1,0:T(8,128)(2,1)}, u32[]{:S(2)}, u32[]{:S(2)}) collective-permute-start(bf16[88,3072]{1,0:T(8,128)(2,1)S(1)} %copy-done.52), channel_id=1, source_target_pairs={{8,0},{16,8},{24,16},{28,24},{20,28},{12,20},{4,12},{0,4},{9,1},{1... | collective-permute-start | bytes 1622024 | tf_op jit(solution)/shard_map/mlp_weights/ppermute | solution.py:45
  50.3 14.2 %collective-permute-start.9 = (bf16[88,3072]{1,0:T(8,128)(2,1)S(1)}, bf16[88,3072]{1,0:T(8,128)(2,1)}, u32[]{:S(2)}, u32[]{:S(2)}) collective-permute-start(bf16[88,3072]{1,0:T(8,128)(2,1)S(1)} %copy-done.52), channel_id=1, source_target_pairs={{0,8},{8,16},{16,24},{24,28},{28,20},{20,12},{12,4},{4,0},{1,9},{9... | collective-permute-start | bytes 1622024 | tf_op jit(solution)/shard_map/mlp_weights/ppermute | solution.py:44
  64.6 33.7 %collective-permute-start.12 = (bf16[88,3072]{1,0:T(8,128)(2,1)}, bf16[88,3072]{1,0:T(8,128)(2,1)S(1)}, u32[]{:S(2)}, u32[]{:S(2)}) collective-permute-start(bf16[88,3072]{1,0:T(8,128)(2,1)} %collective-permute-done.9), channel_id=1, source_target_pairs={{0,8},{8,16},{16,24},{24,28},{28,20},{20,12},{12,4},{4,0},{1,9},{9... | collective-permute-start | bytes 1622024 | tf_op jit(solution)/shard_map/mlp_weights/ppermute | solution.py:44
  66.1 32.1 %collective-permute-start.13 = (bf16[88,3072]{1,0:T(8,128)(2,1)}, bf16[88,3072]{1,0:T(8,128)(2,1)S(1)}, u32[]{:S(2)}, u32[]{:S(2)}) collective-permute-start(bf16[88,3072]{1,0:T(8,128)(2,1)} %collective-permute-done.10), channel_id=1, source_target_pairs={{8,0},{16,8},{24,16},{28,24},{20,28},{12,20},{4,12},{0,4},{9,1},{1... | collective-permute-start | bytes 1622024 | tf_op jit(solution)/shard_map/mlp_weights/ppermute | solution.py:45
  97.1 12.6 %collective-permute-start.11 = (bf16[256,1024]{1,0:T(8,128)(2,1)S(1)}, bf16[256,1024]{1,0:T(8,128)(2,1)S(1)}, u32[]{:S(2)}, u32[]{:S(2)}) collective-permute-start(bf16[256,1024]{1,0:T(8,128)(2,1)S(1)} %multiply_convert_fusion.3), channel_id=1, source_target_pairs={{0,2},{1,3},{2,0},{3,1},{4,6},{5,7},{6,4},{7,5},{8,10},{9,11},{10,... | collective-permute-start | bytes 1572872 | tf_op jit(solution)/shard_map/ppermute | solution.py:165
  98.3 12.9 %collective-permute-start.14 = (bf16[88,3072]{1,0:T(8,128)(2,1)S(1)}, bf16[88,3072]{1,0:T(8,128)(2,1)S(1)}, u32[]{:S(2)}, u32[]{:S(2)}) collective-permute-start(bf16[88,3072]{1,0:T(8,128)(2,1)S(1)} %collective-permute-done.12), channel_id=1, source_target_pairs={{0,8},{8,16},{16,24},{24,28},{28,20},{20,12},{12,4},{4,0},{1,9},{9... | collective-permute-start | bytes 1622024 | tf_op jit(solution)/shard_map/mlp_weights/ppermute | solution.py:44
  99.8 12.5 %collective-permute-start.15 = (bf16[88,3072]{1,0:T(8,128)(2,1)S(1)}, bf16[88,3072]{1,0:T(8,128)(2,1)S(1)}, u32[]{:S(2)}, u32[]{:S(2)}) collective-permute-start(bf16[88,3072]{1,0:T(8,128)(2,1)S(1)} %collective-permute-done.13), channel_id=1, source_target_pairs={{8,0},{16,8},{24,16},{28,24},{20,28},{12,20},{4,12},{0,4},{9,1},{1... | collective-permute-start | bytes 1622024 | tf_op jit(solution)/shard_map/mlp_weights/ppermute | solution.py:45
  101.5 21.2 %collective-permute-start.20 = (bf16[512,1024]{1,0:T(8,128)(2,1)S(1)}, bf16[512,1024]{1,0:T(8,128)(2,1)S(1)}, u32[]{:S(2)}, u32[]{:S(2)}) collective-permute-start(bf16[512,1024]{1,0:T(8,128)(2,1)S(1)} %constant_dynamic-update-slice_fusion.11), channel_id=1, source_target_pairs={{0,1},{1,0},{2,3},{3,2},{4,5},{5,4},{6,7},{7,6},{8,9},{9,8},{10,11... | collective-permute-start | bytes 3145736 | tf_op jit(solution)/shard_map/ppermute | solution.py:165
  112.4 12.2 %collective-permute-start.16 = (bf16[512,1024]{1,0:T(8,128)(2,1)S(1)}, bf16[512,1024]{1,0:T(8,128)(2,1)S(1)}, u32[]{:S(2)}, u32[]{:S(2)}) collective-permute-start(bf16[512,1024]{1,0:T(8,128)(2,1)S(1)} %constant_dynamic-update-slice_fusion), channel_id=1, source_target_pairs={{0,1},{1,0},{2,3},{3,2},{4,5},{5,4},{6,7},{7,6},{8,9},{9,8},{10,11... | collective-permute-start | bytes 3145736 | tf_op jit(solution)/shard_map/ppermute | solution.py:165
  139.2 14.3 %collective-permute-start.23 = (bf16[256,1024]{1,0:T(8,128)(2,1)S(1)}, bf16[256,1024]{1,0:T(8,128)(2,1)S(1)}, u32[]{:S(2)}, u32[]{:S(2)}) collective-permute-start(bf16[256,1024]{1,0:T(8,128)(2,1)S(1)} %slice.432), channel_id=1, source_target_pairs={{0,2},{1,3},{2,0},{3,1},{4,6},{5,7},{6,4},{7,5},{8,10},{9,11},{10,... | collective-permute-start | bytes 1572872 | tf_op jit(solution)/shard_map/ppermute | solution.py:165
  156.8 17.5 %collective-permute-start.24 = (bf16[256,1024]{1,0:T(8,128)(2,1)}, bf16[256,1024]{1,0:T(8,128)(2,1)}, u32[]{:S(2)}, u32[]{:S(2)}) collective-permute-start(bf16[256,1024]{1,0:T(8,128)(2,1)} %slice.351), channel_id=1, source_target_pairs={{0,2},{1,3},{2,0},{3,1},{4,6},{5,7},{6,4},{7,5},{8,10},{9,11},{10,... | collective-permute-start | bytes 1572872 | tf_op jit(solution)/shard_map/ppermute | solution.py:165
  158.8 16.9 %collective-permute-start.27 = (bf16[88,3072]{1,0:T(8,128)(2,1)}, bf16[88,3072]{1,0:T(8,128)(2,1)}, u32[]{:S(2)}, u32[]{:S(2)}) collective-permute-start(bf16[88,3072]{1,0:T(8,128)(2,1)} %get-tuple-element.326), channel_id=1, source_target_pairs={{0,8},{8,16},{16,24},{24,28},{28,20},{20,12},{12,4},{4,0},{1,9},{9... | collective-permute-start | bytes 1622024 | tf_op jit(solution)/shard_map/mlp_grads/ppermute | solution.py:44
  159.2 16.5 %collective-permute-start.28 = (bf16[88,3072]{1,0:T(8,128)(2,1)S(1)}, bf16[88,3072]{1,0:T(8,128)(2,1)}, u32[]{:S(2)}, u32[]{:S(2)}) collective-permute-start(bf16[88,3072]{1,0:T(8,128)(2,1)S(1)} %get-tuple-element.325), channel_id=1, source_target_pairs={{8,0},{16,8},{24,16},{28,24},{20,28},{12,20},{4,12},{0,4},{9,1},{1... | collective-permute-start | bytes 1622024 | tf_op jit(solution)/shard_map/mlp_grads/ppermute | solution.py:45
  177.4 16.4 %collective-permute-start.29 = (bf16[88,3072]{1,0:T(8,128)(2,1)S(1)}, bf16[88,3072]{1,0:T(8,128)(2,1)S(1)}, u32[]{:S(2)}, u32[]{:S(2)}) collective-permute-start(bf16[88,3072]{1,0:T(8,128)(2,1)S(1)} %get-tuple-element.302), channel_id=1, source_target_pairs={{0,8},{8,16},{16,24},{24,28},{28,20},{20,12},{12,4},{4,0},{1,9},{9... | collective-permute-start | bytes 1622024 | tf_op jit(solution)/shard_map/mlp_grads/ppermute | solution.py:44
  177.9 15.9 %collective-permute-start.30 = (bf16[88,3072]{1,0:T(8,128)(2,1)S(1)}, bf16[88,3072]{1,0:T(8,128)(2,1)S(1)}, u32[]{:S(2)}, u32[]{:S(2)}) collective-permute-start(bf16[88,3072]{1,0:T(8,128)(2,1)S(1)} %get-tuple-element.301), channel_id=1, source_target_pairs={{8,0},{16,8},{24,16},{28,24},{20,28},{12,20},{4,12},{0,4},{9,1},{1... | collective-permute-start | bytes 1622024 | tf_op jit(solution)/shard_map/mlp_grads/ppermute | solution.py:45
  195.4 15.7 %collective-permute-start.31 = (bf16[88,3072]{1,0:T(8,128)(2,1)S(1)}, bf16[88,3072]{1,0:T(8,128)(2,1)S(1)}, u32[]{:S(2)}, u32[]{:S(2)}) collective-permute-start(bf16[88,3072]{1,0:T(8,128)(2,1)S(1)} %get-tuple-element.300), channel_id=1, source_target_pairs={{0,8},{8,16},{16,24},{24,28},{28,20},{20,12},{12,4},{4,0},{1,9},{9... | collective-permute-start | bytes 1622024 | tf_op jit(solution)/shard_map/mlp_grads/ppermute | solution.py:44
  196.0 15.2 %collective-permute-start.32 = (bf16[88,3072]{1,0:T(8,128)(2,1)S(1)}, bf16[88,3072]{1,0:T(8,128)(2,1)S(1)}, u32[]{:S(2)}, u32[]{:S(2)}) collective-permute-start(bf16[88,3072]{1,0:T(8,128)(2,1)S(1)} %get-tuple-element.299), channel_id=1, source_target_pairs={{8,0},{16,8},{24,16},{28,24},{20,28},{12,20},{4,12},{0,4},{9,1},{1... | collective-permute-start | bytes 1622024 | tf_op jit(solution)/shard_map/mlp_grads/ppermute | solution.py:45
  212.6 16.7 %collective-permute-start.35 = (bf16[256,1024]{1,0:T(8,128)(2,1)S(1)}, bf16[256,1024]{1,0:T(8,128)(2,1)S(1)}, u32[]{:S(2)}, u32[]{:S(2)}) collective-permute-start(bf16[256,1024]{1,0:T(8,128)(2,1)S(1)} %add_convert_fusion.13), channel_id=1, source_target_pairs={{0,8},{8,16},{16,24},{24,28},{28,20},{20,12},{12,4},{4,0},{1,9},{9... | collective-permute-start | bytes 1572872 | tf_op jit(solution)/shard_map/block_out/ppermute | solution.py:44
  213.3 16.1 %collective-permute-start.36 = (bf16[256,1024]{1,0:T(8,128)(2,1)S(1)}, bf16[256,1024]{1,0:T(8,128)(2,1)S(1)}, u32[]{:S(2)}, u32[]{:S(2)}) collective-permute-start(bf16[256,1024]{1,0:T(8,128)(2,1)S(1)} %add_convert_fusion.13), channel_id=1, source_target_pairs={{8,0},{16,8},{24,16},{28,24},{20,28},{12,20},{4,12},{0,4},{9,1},{1... | collective-permute-start | bytes 1572872 | tf_op jit(solution)/shard_map/block_out/ppermute | solution.py:45
  214.7 14.6 %collective-permute-start.37 = (bf16[256,512]{0,1:T(8,128)(2,1)S(1)}, bf16[256,512]{0,1:T(8,128)(2,1)S(1)}, u32[]{:S(2)}, u32[]{:S(2)}) collective-permute-start(bf16[256,512]{0,1:T(8,128)(2,1)S(1)} %fusion.60), channel_id=1, source_target_pairs={{0,8},{8,16},{16,24},{24,28},{28,20},{20,12},{12,4},{4,0},{1,9},{9... | collective-permute-start | bytes 786440 | tf_op jit(solution)/shard_map/latent_grads/ppermute | solution.py:44
  215.5 17.0 %collective-permute-start.57 = (bf16[256,1024]{1,0:T(8,128)(2,1)S(1)}, bf16[256,1024]{1,0:T(8,128)(2,1)S(1)}, u32[]{:S(2)}, u32[]{:S(2)}) collective-permute-start(bf16[256,1024]{1,0:T(8,128)(2,1)S(1)} %pad_maximum_fusion.8), channel_id=1, source_target_pairs={{0,1},{1,0},{2,3},{3,2},{4,5},{5,4},{6,7},{7,6},{8,9},{9,8},{10,11... | collective-permute-start | bytes 1572872 | tf_op jit(solution)/shard_map/ppermute | solution.py:165
  220.5 28.8 %collective-permute-start.53 = (bf16[1024,512]{1,0:T(8,128)(2,1)S(1)}, bf16[1024,512]{1,0:T(8,128)(2,1)S(1)}, u32[]{:S(2)}, u32[]{:S(2)}) collective-permute-start(bf16[1024,512]{1,0:T(8,128)(2,1)S(1)} %pad_maximum_fusion.2), channel_id=1, source_target_pairs={{0,1},{1,0},{2,3},{3,2},{4,5},{5,4},{6,7},{7,6},{8,9},{9,8},{10,11... | collective-permute-start | bytes 3145736 | tf_op jit(solution)/shard_map/ppermute | solution.py:165
  230.4 16.6 %collective-permute-start.39 = (bf16[256,1024]{1,0:T(8,128)(2,1)S(1)}, bf16[256,1024]{1,0:T(8,128)(2,1)S(1)}, u32[]{:S(2)}, u32[]{:S(2)}) collective-permute-start(bf16[256,1024]{1,0:T(8,128)(2,1)S(1)} %collective-permute-done.35.refs_1_), channel_id=1, source_target_pairs={{0,8},{8,16},{16,24},{24,28},{28,20},{20,12},{12,4},{4,0},{1,9},{9... | collective-permute-start | bytes 1572872 | tf_op jit(solution)/shard_map/block_out/ppermute | solution.py:44
  231.6 15.4 %collective-permute-start.40 = (bf16[256,1024]{1,0:T(8,128)(2,1)S(1)}, bf16[256,1024]{1,0:T(8,128)(2,1)S(1)}, u32[]{:S(2)}, u32[]{:S(2)}) collective-permute-start(bf16[256,1024]{1,0:T(8,128)(2,1)S(1)} %collective-permute-done.36.refs_2_), channel_id=1, source_target_pairs={{8,0},{16,8},{24,16},{28,24},{20,28},{12,20},{4,12},{0,4},{9,1},{1... | collective-permute-start | bytes 1572872 | tf_op jit(solution)/shard_map/block_out/ppermute | solution.py:45
  232.5 14.5 %collective-permute-start.41 = (bf16[256,512]{0,1:T(8,128)(2,1)S(1)}, bf16[256,512]{0,1:T(8,128)(2,1)S(1)}, u32[]{:S(2)}, u32[]{:S(2)}) collective-permute-start(bf16[256,512]{0,1:T(8,128)(2,1)S(1)} %add_convert_fusion.23), channel_id=1, source_target_pairs={{0,8},{8,16},{16,24},{24,28},{28,20},{20,12},{12,4},{4,0},{1,9},{9... | collective-permute-start | bytes 786440 | tf_op jit(solution)/shard_map/latent_grads/ppermute | solution.py:44
  238.8 16.9 %collective-permute-start.58 = (bf16[128,1024]{1,0:T(8,128)(2,1)S(1)}, bf16[128,1024]{1,0:T(8,128)(2,1)S(1)}, u32[]{:S(2)}, u32[]{:S(2)}) collective-permute-start(bf16[128,1024]{1,0:T(8,128)(2,1)S(1)} %slice.452), channel_id=1, source_target_pairs={{0,2},{1,3},{2,0},{3,1},{4,6},{5,7},{6,4},{7,5},{8,10},{9,11},{10,... | collective-permute-start | bytes 786440 | tf_op jit(solution)/shard_map/ppermute | solution.py:165
  259.9 14.9 %collective-permute-start.43 = (bf16[256,1024]{1,0:T(8,128)(2,1)S(1)}, bf16[256,1024]{1,0:T(8,128)(2,1)S(1)}, u32[]{:S(2)}, u32[]{:S(2)}) collective-permute-start(bf16[256,1024]{1,0:T(8,128)(2,1)S(1)} %collective-permute-done.39.refs_3_), channel_id=1, source_target_pairs={{0,8},{8,16},{16,24},{24,28},{28,20},{20,12},{12,4},{4,0},{1,9},{9... | collective-permute-start | bytes 1572872 | tf_op jit(solution)/shard_map/block_out/ppermute | solution.py:44
  260.6 14.9 %collective-permute-start.44 = (bf16[256,1024]{1,0:T(8,128)(2,1)S(1)}, bf16[256,1024]{1,0:T(8,128)(2,1)S(1)}, u32[]{:S(2)}, u32[]{:S(2)}) collective-permute-start(bf16[256,1024]{1,0:T(8,128)(2,1)S(1)} %collective-permute-done.40.refs_4_), channel_id=1, source_target_pairs={{8,0},{16,8},{24,16},{28,24},{20,28},{12,20},{4,12},{0,4},{9,1},{1... | collective-permute-start | bytes 1572872 | tf_op jit(solution)/shard_map/block_out/ppermute | solution.py:45
  265.6 35.6 %collective-permute-start.56 = (bf16[1536,256]{1,0:T(8,128)(2,1)}, bf16[1536,256]{1,0:T(8,128)(2,1)}, u32[]{:S(2)}, u32[]{:S(2)}) collective-permute-start(bf16[1536,256]{1,0:T(8,128)(2,1)} %slice.450), channel_id=1, source_target_pairs={{0,2},{1,3},{2,0},{3,1},{4,6},{5,7},{6,4},{7,5},{8,10},{9,11},{10,... | collective-permute-start | bytes 2359304 | tf_op jit(solution)/shard_map/ppermute | solution.py:165
  266.9 32.2 %collective-permute-start.49 = (bf16[272,1024]{1,0:T(8,128)(2,1)S(1)}, bf16[272,1024]{1,0:T(8,128)(2,1)}, u32[]{:S(2)}, u32[]{:S(2)}) collective-permute-start(bf16[272,1024]{1,0:T(8,128)(2,1)S(1)} %maximum_maximum_fusion.refs_0_), channel_id=1, source_target_pairs={{0,8},{8,16},{16,24},{24,28},{28,20},{20,12},{12,4},{4,0},{1,9},{9... | collective-permute-start | bytes 1671176 | tf_op jit(solution)/shard_map/grad_tokens/ppermute | solution.py:44
  267.9 31.2 %collective-permute-start.50 = (bf16[272,1024]{1,0:T(8,128)(2,1)S(1)}, bf16[272,1024]{1,0:T(8,128)(2,1)}, u32[]{:S(2)}, u32[]{:S(2)}) collective-permute-start(bf16[272,1024]{1,0:T(8,128)(2,1)S(1)} %maximum_maximum_fusion.refs_0_), channel_id=1, source_target_pairs={{8,0},{16,8},{24,16},{28,24},{20,28},{12,20},{4,12},{0,4},{9,1},{1... | collective-permute-start | bytes 1671176 | tf_op jit(solution)/shard_map/grad_tokens/ppermute | solution.py:45
  276.2 15.3 %collective-permute-start.47 = (bf16[256,512]{1,0:T(8,128)(2,1)}, bf16[256,512]{1,0:T(8,128)(2,1)S(1)}, u32[]{:S(2)}, u32[]{:S(2)}) collective-permute-start(bf16[256,512]{1,0:T(8,128)(2,1)} %slice.368), channel_id=1, source_target_pairs={{0,8},{8,16},{16,24},{24,28},{28,20},{20,12},{12,4},{4,0},{1,9},{9... | collective-permute-start | bytes 786440 | tf_op jit(solution)/shard_map/block_out/ppermute | solution.py:44
  277.8 13.8 %collective-permute-start.48 = (bf16[256,512]{1,0:T(8,128)(2,1)}, bf16[256,512]{1,0:T(8,128)(2,1)}, u32[]{:S(2)}, u32[]{:S(2)}) collective-permute-start(bf16[256,512]{1,0:T(8,128)(2,1)} %slice.369), channel_id=1, source_target_pairs={{8,0},{16,8},{24,16},{28,24},{20,28},{12,20},{4,12},{0,4},{9,1},{1... | collective-permute-start | bytes 786440 | tf_op jit(solution)/shard_map/block_out/ppermute | solution.py:45
  287.3 35.2 %all-to-all-start = ((bf16[88,3,1024]{0,1,2:T(4,128)(2,1)}), bf16[88,3,1024]{0,1,2:T(4,128)(2,1)}, u32[]{:S(2)}, u32[]{:S(2)}) async-start(bf16[88,3,1024]{0,1,2:T(4,128)(2,1)} %copy.59), calls=%async_computation | async-start | bytes 2097152 | tf_op jit(solution)/shard_map/all_to_all | solution.py:604
  299.1 15.7 %collective-permute-start.51 = (bf16[272,1024]{1,0:T(8,128)(2,1)}, bf16[272,1024]{1,0:T(8,128)(2,1)S(1)}, u32[]{:S(2)}, u32[]{:S(2)}) collective-permute-start(bf16[272,1024]{1,0:T(8,128)(2,1)} %collective-permute-done.49.refs_1_), channel_id=1, source_target_pairs={{0,8},{8,16},{16,24},{24,28},{28,20},{20,12},{12,4},{4,0},{1,9},{9... | collective-permute-start | bytes 1671176 | tf_op jit(solution)/shard_map/grad_tokens/ppermute | solution.py:44
  300.0 15.8 %collective-permute-start.52 = (bf16[272,1024]{1,0:T(8,128)(2,1)}, bf16[272,1024]{1,0:T(8,128)(2,1)}, u32[]{:S(2)}, u32[]{:S(2)}) collective-permute-start(bf16[272,1024]{1,0:T(8,128)(2,1)} %collective-permute-done.50.refs_2_), channel_id=1, source_target_pairs={{8,0},{16,8},{24,16},{28,24},{20,28},{12,20},{4,12},{0,4},{9,1},{1... | collective-permute-start | bytes 1671176 | tf_op jit(solution)/shard_map/grad_tokens/ppermute | solution.py:45
  303.9 12.5 %collective-permute-start.59 = (bf16[384,128]{1,0:T(8,128)(2,1)S(1)}, bf16[384,128]{1,0:T(8,128)(2,1)S(1)}, u32[]{:S(2)}, u32[]{:S(2)}) collective-permute-start(bf16[384,128]{1,0:T(8,128)(2,1)S(1)} %get-tuple-element.399), channel_id=1, source_target_pairs={{0,8},{8,16},{16,24},{24,28},{28,20},{20,12},{12,4},{4,0},{1,9},{9... | collective-permute-start | bytes 294920 | tf_op jit(solution)/shard_map/attn_grads/ppermute | solution.py:44
  304.8 12.2 %collective-permute-start.60 = (bf16[384,128]{1,0:T(8,128)(2,1)S(1)}, bf16[384,128]{1,0:T(8,128)(2,1)S(1)}, u32[]{:S(2)}, u32[]{:S(2)}) collective-permute-start(bf16[384,128]{1,0:T(8,128)(2,1)S(1)} %get-tuple-element.398), channel_id=1, source_target_pairs={{8,0},{16,8},{24,16},{28,24},{20,28},{12,20},{4,12},{0,4},{9,1},{1... | collective-permute-start | bytes 294920 | tf_op jit(solution)/shard_map/attn_grads/ppermute | solution.py:45
  317.0 18.8 %collective-permute-start.61 = (bf16[272,1024]{1,0:T(8,128)(2,1)S(1)}, bf16[272,1024]{1,0:T(8,128)(2,1)S(1)}, u32[]{:S(2)}, u32[]{:S(2)}) collective-permute-start(bf16[272,1024]{1,0:T(8,128)(2,1)S(1)} %collective-permute-done.51.refs_3_), channel_id=1, source_target_pairs={{0,8},{8,16},{16,24},{24,28},{28,20},{20,12},{12,4},{4,0},{1,9},{9... | collective-permute-start | bytes 1671176 | tf_op jit(solution)/shard_map/grad_tokens/ppermute | solution.py:44
  317.4 18.4 %collective-permute-start.62 = (bf16[272,1024]{1,0:T(8,128)(2,1)}, bf16[272,1024]{1,0:T(8,128)(2,1)S(1)}, u32[]{:S(2)}, u32[]{:S(2)}) collective-permute-start(bf16[272,1024]{1,0:T(8,128)(2,1)} %collective-permute-done.52.refs_4_), channel_id=1, source_target_pairs={{8,0},{16,8},{24,16},{28,24},{20,28},{12,20},{4,12},{0,4},{9,1},{1... | collective-permute-start | bytes 1671176 | tf_op jit(solution)/shard_map/grad_tokens/ppermute | solution.py:45
  319.8 16.0 %collective-permute-start.64 = (bf16[384,256]{1,0:T(8,128)(2,1)}, bf16[384,256]{1,0:T(8,128)(2,1)}, u32[]{:S(2)}, u32[]{:S(2)}) collective-permute-start(bf16[384,256]{1,0:T(8,128)(2,1)} %pad_maximum_fusion.14), channel_id=1, source_target_pairs={{8,0},{16,8},{24,16},{28,24},{20,28},{12,20},{4,12},{0,4},{9,1},{1... | collective-permute-start | bytes 589832 | tf_op jit(solution)/shard_map/attn_grads/ppermute | solution.py:45
  321.7 14.1 %collective-permute-start.63 = (bf16[384,256]{1,0:T(8,128)(2,1)}, bf16[384,256]{1,0:T(8,128)(2,1)}, u32[]{:S(2)}, u32[]{:S(2)}) collective-permute-start(bf16[384,256]{1,0:T(8,128)(2,1)} %pad_maximum_fusion.13), channel_id=1, source_target_pairs={{0,8},{8,16},{16,24},{24,28},{28,20},{20,12},{12,4},{4,0},{1,9},{9... | collective-permute-start | bytes 589832 | tf_op jit(solution)/shard_map/attn_grads/ppermute | solution.py:44
  338.4 10.7 %collective-permute-start.65 = (bf16[272,512]{1,0:T(8,128)(2,1)S(1)}, bf16[272,512]{1,0:T(8,128)(2,1)S(1)}, u32[]{:S(2)}, u32[]{:S(2)}) collective-permute-start(bf16[272,512]{1,0:T(8,128)(2,1)S(1)} %slice.392), channel_id=1, source_target_pairs={{0,8},{8,16},{16,24},{24,28},{28,20},{20,12},{12,4},{4,0},{1,9},{9... | collective-permute-start | bytes 835592 | tf_op jit(solution)/shard_map/grad_tokens/ppermute | solution.py:44
  (131 other events, 1246.9 us)
